TPU v7x, 32 devices: a whole 2x2x4 slice. The times are simulated.
32 devices in a mesh: section: 2 (over core), tensor: 4 (over y, x), dp: 4 (over z).
Axes of the slice: x: 2, y: 2, z: 4, core: 2. Of those that a mesh axis runs over, the one named last changes fastest.
Arguments:
- boundary: bfloat16 [2, 8, 512, 768], P('section', 'dp', 'tensor'), may hold values from -6 to 6
- lengths: int32 [8], P('dp'), may hold values from 128 to 512, as said below
- routes: int32 [2, 8, 512, 2], P('section', 'dp'), may hold values from 0 to 3, all different within a row; in each aligned block of 512 rows (0 to 511, 512 to 1023, ..., all dimensions but the last counted through in order) at most 320 rows name the same one
- attn_gain: float32 [2, 768], P('section'), may hold values from 0.5 to 1.5
- w_query: bfloat16 [2, 768, 768], P('section', None, 'tensor'), may hold values from -0.21875 to 0.21875
- w_key: bfloat16 [2, 768, 768], P('section', None, 'tensor'), may hold values from -0.21875 to 0.21875
- w_value: bfloat16 [2, 768, 768], P('section', None, 'tensor'), may hold values from -0.21875 to 0.21875
- w_out: bfloat16 [2, 768, 768], P('section', 'tensor'), may hold values from -1.25 to 1.25
- ffn_gain: float32 [2, 768], P('section'), may hold values from 0.5 to 1.5
- router: bfloat16 [2, 768, 4], P('section'), may hold values from -0.15625 to 0.15625
- expert_gate: bfloat16 [2, 4, 768, 2048], P('section', None, None, 'tensor'), may hold values from -0.21875 to 0.21875
- expert_up: bfloat16 [2, 4, 768, 2048], P('section', None, None, 'tensor'), may hold values from -0.21875 to 0.21875
- expert_down: bfloat16 [2, 4, 2048, 768], P('section', None, 'tensor'), may hold values from -0.125 to 0.125
- shared_gate: bfloat16 [2, 768, 2048], P('section', None, 'tensor'), may hold values from -0.21875 to 0.21875
- shared_up: bfloat16 [2, 768, 2048], P('section', None, 'tensor'), may hold values from -0.21875 to 0.21875
- shared_down: bfloat16 [2, 2048, 768], P('section', 'tensor'), may hold values from -0.125 to 0.125
Outputs:
- section_outputs: bfloat16 [2, 8, 512, 768], P('section', 'dp', 'tensor')
- section_input_grads: float32 [2, 8, 512, 768], P('section', 'dp', 'tensor')
- attn_gain_grad: float32 [2, 768], P('section')
- w_query_grad: float32 [2, 768, 768], P('section', 'dp', 'tensor')
- w_key_grad: float32 [2, 768, 768], P('section', 'dp', 'tensor')
- w_value_grad: float32 [2, 768, 768], P('section', 'dp', 'tensor')
- w_out_grad: float32 [2, 768, 768], P('section', 'tensor', 'dp')
- ffn_gain_grad: float32 [2, 768], P('section')
- router_grad: float32 [2, 768, 4], P('section')
- expert_gate_grad: float32 [2, 4, 768, 2048], P('section', None, 'dp', 'tensor')
- expert_up_grad: float32 [2, 4, 768, 2048], P('section', None, 'dp', 'tensor')
- expert_down_grad: float32 [2, 4, 2048, 768], P('section', None, 'tensor', 'dp')
- shared_gate_grad: float32 [2, 768, 2048], P('section', 'dp', 'tensor')
- shared_up_grad: float32 [2, 768, 2048], P('section', 'dp', 'tensor')
- shared_down_grad: float32 [2, 2048, 768], P('section', 'tensor', 'dp')
- balance_loss: float32 [2], P('section')
Inputs may be any that keep to these rules, and one draw needn't show every extreme that they name: `lengths`: each group of 2 consecutive sequences holds one of length 512. The two routes of a token differ; within one sequence of one layer no expert is named by more than 320 tokens, a bound that some block reaches.
All inputs are finite; a program needn't handle non-finite values.
Results may differ from a plain program's by a relative error of at most 0.025.
Values may be sent and summed in bfloat16 or wider, within the bound.
A program may use at most 192 MiB of HBM per device.

v0:
```python
import functools

import jax
import jax.numpy as jnp
from jax import lax
from jax.experimental import pallas as pl
from jax.experimental.pallas import tpu as pltpu
from jax.sharding import PartitionSpec as P

HEAD_DIM = 64
HALF_DIM = HEAD_DIM // 2
EPSILON = 1e-06
ALPHA = 0.01
THETA = 10000.0
MASKED = -1e30
LANES = 256
VMEM_LIMIT = 60 * 2**20

f32 = jnp.float32
bf16 = jnp.bfloat16
MESH = pl.DeviceIdType.MESH
ANY = pl.BlockSpec(memory_space=pl.ANY)
VMEM = pl.BlockSpec(memory_space=pltpu.VMEM)
SMEM = pl.BlockSpec(memory_space=pltpu.SMEM)


def dot(left, right, left_dim, right_dim):
    return lax.dot_general(
        left, right, (((left_dim,), (right_dim,)), ((), ())), preferred_element_type=f32
    )


def rope_tables(seq_len):
    frequency = THETA ** (-jnp.arange(HALF_DIM, dtype=f32) / HALF_DIM)
    angles = jnp.arange(seq_len, dtype=jnp.int32).astype(f32)[:, None] * frequency[None, :]
    cosine, sine = jnp.cos(angles), jnp.sin(angles)
    return jnp.concatenate([cosine, cosine, -sine, sine], axis=-1)


def turn_halves(values):
    return jnp.concatenate([values[:, HALF_DIM:], values[:, :HALF_DIM]], axis=1)


class Place:
    def __init__(self, ranks):
        self.s = lax.axis_index("section")
        self.t = lax.axis_index("tensor")
        self.z = lax.axis_index("dp")
        self.ranks = ranks
        self.sibling = (1 - self.s, self.t, self.z)

    def peer(self, k):
        return lax.rem(self.t + k, self.ranks)

    def peer_id(self, k):
        return (self.s, self.peer(k), self.z)

    def greet(self):
        barrier = pltpu.get_barrier_semaphore()
        others = [self.sibling] + [self.peer_id(k) for k in range(1, self.ranks)]
        for other in others:
            pl.semaphore_signal(barrier, inc=1, device_id=other, device_id_type=MESH)
        pl.semaphore_wait(barrier, len(others))


def remote(src, dst, send, recv, device):
    return pltpu.make_async_remote_copy(
        src_ref=src, dst_ref=dst, send_sem=send, recv_sem=recv, device_id=device, device_id_type=MESH
    )


def gather_rows(place, full, rows, send, recv):
    mine = full.at[pl.ds(place.t * rows, rows)]
    copies = []
    for k in range(1, place.ranks):
        copy = remote(mine, mine, send.at[k - 1], recv.at[k - 1], place.peer_id(k))
        copy.start()
        copies.append(copy)
    return copies


def scatter_block(place, stage, landing, rows, lo, width, send, recv):
    copies = []
    for k in range(1, place.ranks):
        src = stage.at[pl.ds(place.peer(k) * rows, rows), pl.ds(lo, width)]
        dst = landing.at[k - 1, :, pl.ds(lo, width)]
        copy = remote(src, dst, send.at[k - 1], recv.at[k - 1], place.peer_id(k))
        copy.start()
        copies.append(copy)
    return copies


def landed_sum(own, landing, ranks):
    total = own
    for k in range(ranks - 1):
        total = total + landing[k].astype(f32)
    return total


def rms_rows(values, gain):
    return values * lax.rsqrt(jnp.mean(values * values, axis=-1, keepdims=True) + EPSILON) * gain


def rms_back(values, gain, grad):
    r = lax.rsqrt(jnp.mean(values * values, axis=-1, keepdims=True) + EPSILON)
    normed = values * r
    scaled = grad * gain
    inner = jnp.mean(scaled * normed, axis=-1, keepdims=True)
    return r * (scaled - normed * inner), jnp.sum(grad * normed, axis=0, keepdims=True)


def column(matrix, index):
    lane = lax.broadcasted_iota(jnp.int32, matrix.shape, 1)
    return jnp.sum(jnp.where(lane == index, matrix, 0.0), axis=1, keepdims=True)


def load_choice(first, pairs, sems):
    for i, (own, other, dst) in enumerate(pairs):

        @pl.when(first)
        def _(own=own, dst=dst, i=i):
            pltpu.make_async_copy(own, dst, sems.at[i]).start()

        @pl.when(jnp.logical_not(first))
        def _(other=other, dst=dst, i=i):
            pltpu.make_async_copy(other, dst, sems.at[i]).start()

    return [pltpu.make_async_copy(own, dst, sems.at[i]) for i, (own, other, dst) in enumerate(pairs)]


N_ATTN = 4
N_FFN = 6


def forward_kernel(
    ranks,
    lens,
    bnd,
    chosen,
    gains,
    router,
    tables,
    *refs,
):
    own = refs[:10]
    refs = refs[10:]
    other = refs[:10]
    (o_gains, o_router, o_chosen, out_rows, cot, probs_sum) = refs[10:16]
    (nf_o, q_o, k_o, v_o, p_o, mx_o, hf_o, g_o, u_o) = refs[16:25]
    (xs, mid, coef, small) = refs[25:29]
    refs = refs[29:]
    (nf, qs, ks, vs, ps, mx, hf, gs, us) = refs[:9]
    refs = refs[9:]
    (wq, wk, wv, wo, wg, wu, wd, acts, stage, land_a, land_f, tmp, own_part, o_bnd, y_low) = refs[:15]
    (ag_s, ag_r, rsa_s, rsa_r, rsf_s, rsf_r, ex_s, ex_r, load_sem, save_sem, row_s, row_r) = refs[15:]

    place = Place(ranks)
    s, t = place.s, place.t
    rows, width = bnd.shape[1], bnd.shape[2]
    seq_len = nf.shape[1]
    experts = wg.shape[0] - 1
    heads = qs.shape[1]
    mine = pl.ds(t * rows, rows)
    place.greet()

    ex_pairs = [
        (bnd.at[1 - s], o_bnd),
        (gains, o_gains),
        (router, o_router),
        (chosen.at[1 - s], o_chosen),
    ] + [(own[i], other[i]) for i in range(10)]
    exchange = [
        remote(src, dst, ex_s.at[i], ex_r.at[i], place.sibling) for i, (src, dst) in enumerate(ex_pairs)
    ]
    for copy in exchange:
        copy.start()
    for copy in exchange[:4]:
        copy.wait()
    is_first = s == 0
    xs[0] = jnp.where(is_first, bnd[0], o_bnd[...])
    cot[...] = jnp.where(is_first, o_bnd[...], bnd[1])
    length = lens[s]

    ffn_targets = [
        (wg.at[pl.ds(0, experts)]),
        (wu.at[pl.ds(0, experts)]),
        (wd.at[pl.ds(0, experts)]),
        wg.at[experts],
        wu.at[experts],
        wd.at[experts],
    ]
    attn_targets = [wq, wk, wv, wo]

    def layer(l, carry):
        here = s == l
        gain_a = jnp.where(here, gains[0:1], o_gains[0:1])
        gain_f = jnp.where(here, gains[1:2], o_gains[1:2])
        x = xs[l].astype(f32)
        nf[l, mine] = rms_rows(x, gain_a).astype(bf16)
        ag = gather_rows(place, nf.at[l], rows, ag_s.at[l, 0], ag_r.at[l, 0])

        @pl.when(jnp.logical_not(here))
        def _():
            for copy in exchange[4 : 4 + N_ATTN]:
                copy.wait_recv()

        loads = load_choice(
            here, [(own[i], other[i], attn_targets[i]) for i in range(N_ATTN)], load_sem
        )

        @pl.when(jnp.logical_not(here))
        def _():
            for copy in exchange[4 + N_ATTN :]:
                copy.wait_recv()

        ffn_loads = load_choice(
            here,
            [(own[4 + i], other[4 + i], ffn_targets[i]) for i in range(N_FFN)],
            load_sem.at[pl.ds(N_ATTN, N_FFN)],
        )
        for copy in loads:
            copy.wait()
        for copy in ag:
            copy.wait()
        pltpu.make_async_copy(nf.at[l], nf_o.at[l], save_sem.at[l, 0]).start()
        cosine, signed = tables[:, :HEAD_DIM], tables[:, HEAD_DIM:]
        normed = nf[l]
        for w, dst, turned in ((wq, qs, True), (wk, ks, True), (wv, vs, False)):
            projected = dot(normed, w[...], 1, 0)
            for h in range(heads):
                piece = projected[:, h * HEAD_DIM : (h + 1) * HEAD_DIM]
                if turned:
                    piece = piece * cosine + turn_halves(piece) * signed
                dst[l, h] = piece.astype(bf16)
        scat = []
        for i in range(ranks):
            lo, reach = i * rows, (i + 1) * rows
            place_q = lax.broadcasted_iota(jnp.int32, (rows, reach), 0) + lo
            place_k = lax.broadcasted_iota(jnp.int32, (rows, reach), 1)
            allowed = (place_k <= place_q) & (place_k < length)
            for h in range(heads):
                scores = dot(qs[l, h, lo:reach], ks[l, h, 0:reach], 1, 1) * HEAD_DIM ** (-0.5)
                scores = jnp.where(allowed, scores, MASKED)
                peak = jnp.max(scores, axis=-1, keepdims=True)
                raised = jnp.exp(scores - peak)
                total = jnp.sum(raised, axis=-1, keepdims=True)
                weights = (raised / total).astype(bf16)
                ps[l, h, lo:reach, 0:reach] = weights
                if reach < seq_len:
                    ps[l, h, lo:reach, reach:] = jnp.zeros((rows, seq_len - reach), bf16)
                mixed = dot(weights, vs[l, h, 0:reach], 1, 0)
                mx[l, lo:reach, h * HEAD_DIM : (h + 1) * HEAD_DIM] = mixed.astype(bf16)
            part = dot(mx[l, lo:reach], wo[...], 1, 0)
            stage[lo:reach] = part.astype(bf16)

            @pl.when(t == i)
            def _(part=part):
                own_part[...] = part

            @pl.when(t != i)
            def _(i=i, lo=lo):
                k = lax.rem(i - t + ranks, ranks)
                remote(
                    stage.at[pl.ds(lo, rows)],
                    land_a.at[l, k - 1],
                    rsa_s.at[l, k - 1],
                    rsa_r.at[l, k - 1],
                    (s, i, place.z),
                ).start()

        saves = [(qs, q_o), (ks, k_o), (vs, v_o), (ps, p_o), (mx, mx_o)]
        for i, (src, dst) in enumerate(saves):
            pltpu.make_async_copy(src.at[l], dst.at[l], save_sem.at[l, 1 + i]).start()
        for k in range(1, ranks):
            remote(
                stage.at[pl.ds(place.peer(k) * rows, rows)],
                land_a.at[l, k - 1],
                rsa_s.at[l, k - 1],
                rsa_r.at[l, k - 1],
                place.peer_id(k),
            ).wait()
        middle = x + landed_sum(own_part[...], land_a.at[l], ranks)
        mid[l] = middle
        hf[l, mine] = rms_rows(middle, gain_f).astype(bf16)
        ag = gather_rows(place, hf.at[l], rows, ag_s.at[l, 1], ag_r.at[l, 1])
        for copy in ffn_loads:
            copy.wait()
        for copy in ag:
            copy.wait()
        pltpu.make_async_copy(hf.at[l], hf_o.at[l], save_sem.at[l, 6]).start()
        hidden = hf[l]
        route_w = jnp.where(here, router[...], o_router[...])
        names = jnp.where(here, chosen[s], o_chosen[...])
        logits = dot(route_w, hidden, 1, 1)
        expert_row = lax.broadcasted_iota(jnp.int32, logits.shape, 0)
        logits = jnp.where(expert_row < experts, logits, MASKED)
        raised = jnp.exp(logits - jnp.max(logits, axis=0, keepdims=True))
        raised = jnp.where(expert_row < experts, raised, 0.0)
        chances = raised / jnp.sum(raised, axis=0, keepdims=True)
        per_chosen = names / jnp.sum(chances * names, axis=0, keepdims=True)
        gates = chances * per_chosen
        small[l, 0:8] = chances
        small[l, 8:16] = gates
        small[l, 16:24] = per_chosen
        token = lax.broadcasted_iota(jnp.int32, logits.shape, 1)
        summed = jnp.sum(jnp.where(token < length, chances, 0.0), axis=1, keepdims=True)
        probs_sum[l] = jnp.broadcast_to(summed, (8, 128))
        coef[l] = jnp.where(expert_row == experts, 1.0, gates).T

        def one_expert(e, carry):
            gate_h = dot(hf[l], wg[e], 1, 0)
            up_h = dot(hf[l], wu[e], 1, 0)
            gs[l, e] = gate_h.astype(bf16)
            us[l, e] = up_h.astype(bf16)
            weight = column(coef[l], e)
            acts[e] = (gate_h * jax.nn.sigmoid(gate_h) * up_h * weight).astype(bf16)
            return carry

        lax.fori_loop(0, experts + 1, one_expert, 0)
        pltpu.make_async_copy(gs.at[l], g_o.at[l], save_sem.at[l, 7]).start()
        pltpu.make_async_copy(us.at[l], u_o.at[l], save_sem.at[l, 8]).start()
        scat = []
        for n in range(width // LANES):
            lanes = slice(n * LANES, (n + 1) * LANES)
            total = dot(acts[0], wd[0, :, lanes], 1, 0)
            for e in range(1, experts + 1):
                total = total + dot(acts[e], wd[e, :, lanes], 1, 0)
            tmp[...] = total
            stage[:, lanes] = total.astype(bf16)
            own_part[:, lanes] = tmp[mine]
            scat += scatter_block(
                place, stage, land_f.at[l], rows, n * LANES, LANES, rsf_s.at[l, n], rsf_r.at[l, n]
            )
        for copy in scat:
            copy.wait()
        output = mid[l] + landed_sum(own_part[...], land_f.at[l], ranks)
        y_low[l] = output.astype(bf16)
        xs[1] = jnp.where(l == 0, y_low[l], xs[1])

        @pl.when(here)
        def _():
            out_rows[s] = y_low[l]

        @pl.when(jnp.logical_not(here))
        def _():
            remote(y_low.at[l], out_rows.at[s], row_s, row_r, place.sibling).start()

        return carry

    xs[1] = jnp.zeros_like(xs[1])
    lax.fori_loop(0, 2, layer, 0)
    remote(y_low.at[1 - s], out_rows.at[s], row_s, row_r, place.sibling).wait_send()
    remote(y_low.at[1 - s], out_rows.at[1 - s], row_s, row_r, place.sibling).wait_recv()
    for copy in exchange[4:]:
        copy.wait_send()
    pairs = [(nf, nf_o), (qs, q_o), (ks, k_o), (vs, v_o), (ps, p_o), (mx, mx_o), (hf, hf_o), (gs, g_o), (us, u_o)]
    for l in range(2):
        for i, (src, dst) in enumerate(pairs):
            pltpu.make_async_copy(src.at[l], dst.at[l], save_sem.at[l, i]).wait()


def ffn_back_kernel(l, ranks, *refs):
    (lens, dy_in, aux, gains, o_gains, router, o_router, mid, coef, small, hf_i, g_i, u_i) = refs[:13]
    own, other = refs[13:19], refs[19:25]
    (d_mid, grads, gain_grad, router_grad) = refs[25:29]
    (hf, gs, us, wg, wu, wd, dyf, acts, stage, land, tmp, own_part, gate_sum, sent, got) = refs[29:44]
    (ag_s, ag_r, rs_s, rs_r, ex_s, ex_r, load_sem, st_sem) = refs[44:]

    place = Place(ranks)
    s, t = place.s, place.t
    rows, width = dy_in.shape
    seq_len = hf.shape[0]
    experts = wg.shape[0] - 1
    inner = wg.shape[2]
    half = inner // 2
    mine = pl.ds(t * rows, rows)
    here = s == l
    state = [
        pltpu.make_async_copy(src.at[l], dst, st_sem.at[i])
        for i, (src, dst) in enumerate([(g_i, gs), (u_i, us), (hf_i, hf)])
    ]
    targets = [
        wg.at[pl.ds(0, experts)],
        wu.at[pl.ds(0, experts)],
        wd.at[pl.ds(0, experts)],
        wg.at[experts],
        wu.at[experts],
        wd.at[experts],
    ]
    order = (2, 5, 0, 1, 3, 4)
    loads = load_choice(here, [(own[i], other[i], targets[i]) for i in order], load_sem)
    for copy in state:
        copy.start()
    dy = dy_in[...]
    if l == 1:
        position = lax.broadcasted_iota(jnp.int32, (rows, width), 0) + t * rows
        dy = jnp.where(position < lens[s], dy.astype(f32), 0.0).astype(bf16)
    dyf[mine] = dy
    place.greet()
    ag = gather_rows(place, dyf, rows, ag_s, ag_r)
    for copy in loads:
        copy.wait()
    for copy in state:
        copy.wait()
    gate_sum[...] = jnp.zeros_like(gate_sum)
    for copy in ag:
        copy.wait()
    lane8 = lax.broadcasted_iota(jnp.int32, gate_sum.shape, 1)

    def one_expert(e, carry):
        raw = dot(dyf[...], wd[e], 1, 1)
        gate_h = gs[e].astype(f32)
        up_h = us[e].astype(f32)
        sig = jax.nn.sigmoid(gate_h)
        silu = gate_h * sig
        acted = silu * up_h
        inner_sum = jnp.sum(acted * raw, axis=1, keepdims=True)
        gate_sum[...] = jnp.where(lane8 == e, inner_sum, gate_sum[...])
        weight = column(coef[l], e)
        acts[e] = (acted * weight).astype(bf16)
        d_acted = raw * weight
        gs[e] = (d_acted * up_h * (sig + silu * (1.0 - sig))).astype(bf16)
        us[e] = (d_acted * silu).astype(bf16)
        return carry

    lax.fori_loop(0, experts + 1, one_expert, 0)
    chances, gates, per_chosen = small[l, 0:8], small[l, 8:16], small[l, 16:24]
    d_gates = gate_sum[...].T
    common = jnp.sum(d_gates * gates, axis=0, keepdims=True)
    d_chances = per_chosen * (d_gates - common) + jnp.where(t == 0, aux[l], 0.0)
    d_logits = chances * (d_chances - jnp.sum(chances * d_chances, axis=0, keepdims=True))
    d_logits = d_logits.astype(bf16)
    router_grad[...] = dot(d_logits, hf[...], 1, 0)
    route_w = jnp.where(here, router[...], o_router[...])
    scat = []
    for n in range(width // LANES):
        lanes = slice(n * LANES, (n + 1) * LANES)
        total = dot(d_logits, route_w[:, lanes], 0, 0)
        for e in range(experts + 1):
            total = total + dot(gs[e], wg[e, lanes], 1, 1)
            total = total + dot(us[e], wu[e, lanes], 1, 1)
        tmp[...] = total
        stage[:, lanes] = total.astype(bf16)
        own_part[:, lanes] = tmp[mine]
        scat += scatter_block(place, stage, land, rows, n * LANES, LANES, rs_s.at[n], rs_r.at[n])

    theirs = pl.ds(pl.multiple_of((1 - s) * half, half), half)
    ours = pl.ds(pl.multiple_of(s * half, half), half)
    sources = ((hf, gs), (hf, us), (dyf, acts))

    def give(e, carry):
        for j, (left, right) in enumerate(sources):
            sent[e * 3 + j] = dot(left[...], right[e, :, theirs], 0, 0).astype(bf16)
            at = e * 3 + j
            remote(sent.at[at], got.at[at], ex_s.at[at], ex_r.at[at], place.sibling).start()
        return carry

    lax.fori_loop(0, experts + 1, give, 0)
    for copy in scat:
        copy.wait()
    d_hidden = landed_sum(own_part[...], land, ranks)
    gain_f = jnp.where(here, gains[1:2], o_gains[1:2])
    d_norm, g_gain = rms_back(mid[l], gain_f, d_hidden)
    d_mid[...] = dyf[mine].astype(f32) + d_norm
    gain_grad[...] = g_gain

    def keep(e, carry):
        for j, (left, right) in enumerate(sources):
            at = e * 3 + j
            value = dot(left[...], right[e, :, ours], 0, 0)
            remote(sent.at[at], got.at[at], ex_s.at[at], ex_r.at[at], place.sibling).wait()
            lanes = pl.ds(pl.multiple_of((j * (experts + 1) + e) * half, half), half)
            grads[:, lanes] = (value + got[at].astype(f32)).astype(bf16)
        return carry

    lax.fori_loop(0, experts + 1, keep, 0)


def attn_back_kernel(l, ranks, *refs):
    (d_mid, gains, o_gains, tables, xs, nf_i, q_i, k_i, v_i, p_i, mx_i) = refs[:11]
    own, other = refs[11:15], refs[15:19]
    (dx_low, in_grads, grads, gain_grad) = refs[19:23]
    (nf, qs, ks, vs, ps, mx, wq, wk, wv, wo, df, ds, dq, dk, dv, stage, land, tmp, own_part) = refs[23:42]
    (gw, got, row_buf, ag_s, ag_r, rs_s, rs_r, ex_s, ex_r, load_sem, st_sem, row_s, row_r) = refs[42:]

    place = Place(ranks)
    s, t = place.s, place.t
    rows, width = d_mid.shape
    seq_len = nf.shape[0]
    heads = qs.shape[0]
    mine = pl.ds(t * rows, rows)
    here = s == l
    targets = [wq, wk, wv, wo]
    loads = load_choice(here, [(own[i], other[i], targets[i]) for i in range(N_ATTN)], load_sem)
    pairs = [(nf_i, nf), (q_i, qs), (k_i, ks), (v_i, vs), (p_i, ps), (mx_i, mx)]
    state = [pltpu.make_async_copy(src.at[l], dst, st_sem.at[i]) for i, (src, dst) in enumerate(pairs)]
    for copy in state:
        copy.start()
    df[mine] = d_mid[...].astype(bf16)
    place.greet()
    ag = gather_rows(place, df, rows, ag_s, ag_r)
    for copy in loads:
        copy.wait()
    for copy in state:
        copy.wait()
    for copy in ag:
        copy.wait()
    cosine, signed = tables[:, :HEAD_DIM], tables[:, HEAD_DIM:]
    scale = HEAD_DIM ** (-0.5)
    for h in range(heads):
        span = slice(h * HEAD_DIM, (h + 1) * HEAD_DIM)
        d_mixed = dot(df[...], wo[span], 1, 1).astype(bf16)
        for i in range(ranks):
            lo, reach = i * rows, (i + 1) * rows
            weights = ps[h, lo:reach, 0:reach].astype(f32)
            d_probs = dot(d_mixed[lo:reach], vs[h, 0:reach], 1, 1)
            inner = jnp.sum(weights * d_probs, axis=-1, keepdims=True)
            ds[lo:reach, 0:reach] = (weights * (d_probs - inner)).astype(bf16)
            if reach < seq_len:
                ds[lo:reach, reach:] = jnp.zeros((rows, seq_len - reach), bf16)
        d_value = dot(ps[h], d_mixed, 0, 0)
        d_query = dot(ds[...], ks[h], 1, 0) * scale
        d_key = dot(ds[...], qs[h], 0, 0) * scale
        dq[:, span] = (d_query * cosine - turn_halves(d_query) * signed).astype(bf16)
        dk[:, span] = (d_key * cosine - turn_halves(d_key) * signed).astype(bf16)
        dv[:, span] = d_value.astype(bf16)
    scat = []
    for n in range(width // LANES):
        lanes = slice(n * LANES, (n + 1) * LANES)
        total = dot(dq[...], wq[lanes], 1, 1) + dot(dk[...], wk[lanes], 1, 1) + dot(dv[...], wv[lanes], 1, 1)
        tmp[...] = total
        stage[:, lanes] = total.astype(bf16)
        own_part[:, lanes] = tmp[mine]
        scat += scatter_block(place, stage, land, rows, n * LANES, LANES, rs_s.at[n], rs_r.at[n])
    for j, (left, right) in enumerate(((nf, dq), (nf, dk), (nf, dv), (df, mx))):
        gw[j] = dot(left[...], right[...], 0, 0).astype(bf16)
    swap = remote(gw.at[pl.ds((1 - s) * 2, 2)], got, ex_s, ex_r, place.sibling)
    swap.start()
    for copy in scat:
        copy.wait()
    d_normed = landed_sum(own_part[...], land, ranks)
    gain_a = jnp.where(here, gains[0:1], o_gains[0:1])
    d_norm, g_gain = rms_back(xs[l].astype(f32), gain_a, d_normed)
    dx = d_mid[...] + d_norm
    gain_grad[...] = g_gain
    low = dx.astype(bf16)
    dx_low[...] = low
    row_buf[...] = low.astype(f32) if l == 1 else dx

    @pl.when(here)
    def _():
        in_grads[s] = row_buf[...]
        remote(row_buf, in_grads.at[1 - s], row_s, row_r, place.sibling).wait_recv()

    @pl.when(jnp.logical_not(here))
    def _():
        copy = remote(row_buf, in_grads.at[s], row_s, row_r, place.sibling)
        copy.start()
        copy.wait_send()

    swap.wait()
    for j in range(2):
        grads[j] = (gw[2 * s + j].astype(f32) + got[j].astype(f32)).astype(bf16)


def params(collective_id):
    return pltpu.CompilerParams(
        collective_id=collective_id, has_side_effects=True, vmem_limit_bytes=VMEM_LIMIT
    )


def shape_of(*dims, dtype=bf16):
    return jax.ShapeDtypeStruct(dims, dtype)


def on_device(ranks, *args):
    (boundary, lengths, routes, attn_gain, w_query, w_key, w_value, w_out, ffn_gain, router) = args[:10]
    ffn_own = tuple(a[0] for a in args[10:])
    attn_own = (w_query[0], w_key[0], w_value[0], w_out[0])
    section = lax.axis_index("section")
    first_section = section == 0
    rows, width = boundary.shape[2:]
    seqs, seq_len = routes.shape[1:3]
    top = routes.shape[3]
    experts, _, inner = ffn_own[0].shape
    blocks = experts + 1
    heads_width = w_query.shape[2]
    heads = heads_width // HEAD_DIM
    chunks = width // LANES
    half = inner // 2
    dma = pltpu.SemaphoreType.DMA

    expert_ids = jnp.arange(8, dtype=jnp.int32)
    chosen = jnp.any(routes[0][:, None, :, :] == expert_ids[None, :, None, None], axis=-1).astype(f32)
    valid = (jnp.arange(seq_len, dtype=jnp.int32)[None, :] < lengths[:, None]).astype(f32)
    counts_here = jnp.sum(chosen * valid[:, None, :], axis=(0, 2))
    counts_placed = jnp.where(section == jnp.arange(2)[:, None], counts_here[None, :], 0.0)
    counts, doubled = lax.psum(
        (counts_placed, jnp.sum(lengths).astype(f32)), ("section", "dp")
    )
    tokens_all = doubled / 2.0
    share = counts / (top * tokens_all)
    own_valid = jnp.where(first_section, valid[0], valid[1])
    aux = (ALPHA * experts / tokens_all) * share[:, :, None] * own_valid[None, None, :]

    gains = jnp.concatenate([attn_gain, ffn_gain], axis=0)
    router_t = jnp.pad(router[0].T, ((0, 8 - experts), (0, 0)))
    tables = rope_tables(seq_len)

    states = [
        shape_of(2, seq_len, width),
        shape_of(2, heads, seq_len, HEAD_DIM),
        shape_of(2, heads, seq_len, HEAD_DIM),
        shape_of(2, heads, seq_len, HEAD_DIM),
        shape_of(2, heads, seq_len, seq_len),
        shape_of(2, seq_len, heads_width),
        shape_of(2, seq_len, width),
        shape_of(2, blocks, seq_len, inner),
        shape_of(2, blocks, seq_len, inner),
    ]
    weights = attn_own + ffn_own
    ffn_scratch = [
        pltpu.VMEM((blocks, width, inner), bf16),
        pltpu.VMEM((blocks, width, inner), bf16),
        pltpu.VMEM((blocks, inner, width), bf16),
    ]
    attn_scratch = [
        pltpu.VMEM((width, heads_width), bf16),
        pltpu.VMEM((width, heads_width), bf16),
        pltpu.VMEM((width, heads_width), bf16),
        pltpu.VMEM((heads_width, width), bf16),
    ]
    peers = ranks - 1
    result = pl.pallas_call(
        functools.partial(forward_kernel, ranks),
        out_shape=[shape_of(*w.shape) for w in weights]
        + [
            shape_of(2, width, dtype=f32),
            shape_of(8, width),
            shape_of(8, seq_len, dtype=f32),
            shape_of(2, rows, width),
            shape_of(rows, width),
            shape_of(2, 8, 128, dtype=f32),
        ]
        + states
        + [
            shape_of(2, rows, width),
            shape_of(2, rows, width, dtype=f32),
            shape_of(2, seq_len, 8, dtype=f32),
            shape_of(2, 24, seq_len, dtype=f32),
        ],
        in_specs=[SMEM] + [VMEM] * 5 + [ANY] * 10,
        out_specs=[ANY] * 10 + [VMEM] * 6 + [ANY] * 9 + [VMEM] * 4,
        scratch_shapes=[pltpu.VMEM(st.shape, st.dtype) for st in states]
        + attn_scratch
        + ffn_scratch
        + [
            pltpu.VMEM((blocks, seq_len, inner), bf16),
            pltpu.VMEM((seq_len, width), bf16),
            pltpu.VMEM((2, peers, rows, width), bf16),
            pltpu.VMEM((2, peers, rows, width), bf16),
            pltpu.VMEM((seq_len, LANES), f32),
            pltpu.VMEM((rows, width), f32),
            pltpu.VMEM((rows, width), bf16),
            pltpu.VMEM((2, rows, width), bf16),
            dma((2, 2, peers)),
            dma((2, 2, peers)),
            dma((2, peers)),
            dma((2, peers)),
            dma((2, chunks, peers)),
            dma((2, chunks, peers)),
            dma((14,)),
            dma((14,)),
            dma((10,)),
            dma((2, 9)),
            dma,
            dma,
        ],
        compiler_params=params(0),
        name="forward",
    )(lengths, boundary[0], chosen, gains, router_t, tables, *weights)
    other = result[:10]
    (o_gains, o_router, _, out_rows, cot, probs_sum) = result[10:16]
    (nf, qs, ks, vs, ps, mx, hf, gs, us) = result[16:25]
    (xs, mid, coef, small) = result[25:29]

    def ffn_back(l, dy):
        return pl.pallas_call(
            functools.partial(ffn_back_kernel, l, ranks),
            out_shape=[
                shape_of(rows, width, dtype=f32),
                shape_of(width, 3 * blocks * half),
                shape_of(1, width, dtype=f32),
                shape_of(8, width, dtype=f32),
            ],
            in_specs=[SMEM] + [VMEM] * 9 + [ANY] * 15,
            out_specs=[VMEM] * 4,
            scratch_shapes=[
                pltpu.VMEM((seq_len, width), bf16),
                pltpu.VMEM((blocks, seq_len, inner), bf16),
                pltpu.VMEM((blocks, seq_len, inner), bf16),
            ]
            + ffn_scratch
            + [
                pltpu.VMEM((seq_len, width), bf16),
                pltpu.VMEM((blocks, seq_len, inner), bf16),
                pltpu.VMEM((seq_len, width), bf16),
                pltpu.VMEM((peers, rows, width), bf16),
                pltpu.VMEM((seq_len, LANES), f32),
                pltpu.VMEM((rows, width), f32),
                pltpu.VMEM((seq_len, 8), f32),
                pltpu.VMEM((3 * blocks, width, half), bf16),
                pltpu.VMEM((3 * blocks, width, half), bf16),
                dma((peers,)),
                dma((peers,)),
                dma((chunks, peers)),
                dma((chunks, peers)),
                dma((3 * blocks,)),
                dma((3 * blocks,)),
                dma((6,)),
                dma((3,)),
            ],
            compiler_params=params(1 + l),
            name=f"ffn_back_{l}",
        )(lengths, dy, aux, gains, o_gains, router_t, o_router, mid, coef, small, hf, gs, us, *ffn_own, *other[4:])

    def attn_back(l, d_mid):
        return pl.pallas_call(
            functools.partial(attn_back_kernel, l, ranks),
            out_shape=[
                shape_of(rows, width),
                shape_of(seqs, rows, width, dtype=f32),
                shape_of(2, width, heads_width),
                shape_of(1, width, dtype=f32),
            ],
            in_specs=[VMEM] * 5 + [ANY] * 14,
            out_specs=[VMEM] * 4,
            scratch_shapes=[pltpu.VMEM(st.shape[1:], st.dtype) for st in states[:6]]
            + attn_scratch
            + [
                pltpu.VMEM((seq_len, width), bf16),
                pltpu.VMEM((seq_len, seq_len), bf16),
                pltpu.VMEM((seq_len, heads_width), bf16),
                pltpu.VMEM((seq_len, heads_width), bf16),
                pltpu.VMEM((seq_len, heads_width), bf16),
                pltpu.VMEM((seq_len, width), bf16),
                pltpu.VMEM((peers, rows, width), bf16),
                pltpu.VMEM((seq_len, LANES), f32),
                pltpu.VMEM((rows, width), f32),
                pltpu.VMEM((4, width, heads_width), bf16),
                pltpu.VMEM((2, width, heads_width), bf16),
                pltpu.VMEM((rows, width), f32),
                dma((peers,)),
                dma((peers,)),
                dma((chunks, peers)),
                dma((chunks, peers)),
                dma,
                dma,
                dma((4,)),
                dma((6,)),
                dma,
                dma,
            ],
            compiler_params=params(3 + l),
            name=f"attn_back_{l}",
        )(d_mid, gains, o_gains, tables, xs, nf, qs, ks, vs, ps, mx, *attn_own, *other[:4])

    def over_dp(array, dim):
        return lax.psum_scatter(array, "dp", scatter_dimension=dim, tiled=True)

    d_mid_1, ffn_grads_1, ffn_gain_1, router_1 = ffn_back(1, cot)
    ffn_done_1 = over_dp(ffn_grads_1, 0)
    dx_low_1, in_grads_1, attn_grads_1, attn_gain_1 = attn_back(1, d_mid_1)
    attn_done_1 = over_dp(attn_grads_1, 1)
    d_mid_0, ffn_grads_0, ffn_gain_0, router_0 = ffn_back(0, dx_low_1)
    ffn_done_0 = over_dp(ffn_grads_0, 0)
    _, in_grads_0, attn_grads_0, attn_gain_0 = attn_back(0, d_mid_0)
    attn_done_0 = over_dp(attn_grads_0, 1)

    tensor_first = (lax.axis_index("tensor") == 0).astype(f32)
    small_sums = lax.psum(
        jnp.stack(
            [
                jnp.concatenate([attn_gain_0, ffn_gain_0, router_0], axis=0),
                jnp.concatenate([attn_gain_1, ffn_gain_1, router_1], axis=0),
            ]
        ),
        ("section", "tensor", "dp"),
    )
    prob_sum = lax.psum(probs_sum[:, :, 0] * tensor_first, ("section", "tensor", "dp"))
    here_sums = jnp.where(first_section, small_sums[0], small_sums[1])
    here_prob = jnp.where(first_section, prob_sum[0], prob_sum[1])
    here_share = jnp.where(first_section, share[0], share[1])
    balance = (experts * jnp.sum(here_share * here_prob) / tokens_all).reshape(1)

    def swap(first, second):
        mine = jnp.where(first_section, first, second)
        theirs = lax.ppermute(jnp.where(first_section, second, first), "section", [(0, 1), (1, 0)])
        return jnp.where(first_section, mine, theirs), jnp.where(first_section, theirs, mine)

    low_half, high_half = swap(ffn_done_0, ffn_done_1)
    part = low_half.shape[0]
    shaped = [h.reshape(part, 3, blocks, half) for h in (low_half, high_half)]
    merged = jnp.concatenate(shaped, axis=-1).astype(f32)
    expert_gate = merged[:, 0, :experts].transpose(1, 0, 2)
    expert_up = merged[:, 1, :experts].transpose(1, 0, 2)
    expert_down = merged[:, 2, :experts].transpose(1, 2, 0)
    shared_gate, shared_up = merged[:, 0, experts], merged[:, 1, experts]
    shared_down = merged[:, 2, experts].T
    qk, vo = swap(attn_done_0, attn_done_1)
    qk, vo = qk.astype(f32), vo.astype(f32)
    in_grads = jnp.where(first_section, in_grads_0, in_grads_1)
    return (
        out_rows[None],
        in_grads[None],
        here_sums[0][None],
        qk[0][None],
        qk[1][None],
        vo[0][None],
        vo[1].T[None],
        here_sums[1][None],
        here_sums[2 : 2 + experts].T[None],
        expert_gate[None],
        expert_up[None],
        expert_down[None],
        shared_gate[None],
        shared_up[None],
        shared_down[None],
        balance,
    )


def solution(mesh):
    placed = (
        P("section", "dp", "tensor", None),
        P("dp"),
        P("section", "dp", None, None),
        P("section", None),
        P("section", None, "tensor"),
        P("section", None, "tensor"),
        P("section", None, "tensor"),
        P("section", "tensor", None),
        P("section", None),
        P("section", None, None),
        P("section", None, None, "tensor"),
        P("section", None, None, "tensor"),
        P("section", None, "tensor", None),
        P("section", None, "tensor"),
        P("section", None, "tensor"),
        P("section", "tensor", None),
    )
    return jax.shard_map(
        functools.partial(on_device, mesh.shape["tensor"]),
        mesh=mesh,
        in_specs=placed,
        out_specs=(
            P("section", "dp", "tensor", None),
            P("section", "dp", "tensor", None),
            P("section", None),
            P("section", "dp", "tensor"),
            P("section", "dp", "tensor"),
            P("section", "dp", "tensor"),
            P("section", "tensor", "dp"),
            P("section", None),
            P("section", None, None),
            P("section", None, "dp", "tensor"),
            P("section", None, "dp", "tensor"),
            P("section", None, "tensor", "dp"),
            P("section", "dp", "tensor"),
            P("section", "dp", "tensor"),
            P("section", "tensor", "dp"),
            P("section"),
        ),
        check_vma=False,
    )
```

profile of v0, /device:TPU:0, one launch (start us, length us, event | category | flops | bytes accessed | tf_op | source)
XLA Modules:
  0.0 496.6 jit_solution(109442479383559319)
XLA Ops:
  7.2 0.0 reduce-scatter.11.cloned.1.call-start
  7.3 1.3 reduce_sum.27
  8.6 0.7 compare_convert_fusion
  10.0 0.7 fusion.1
  10.7 0.6 convert_element_type.40.chosen
  11.3 0.1 select_reduce_fusion
  11.4 1.9 copy.65
  13.3 1.9 copy.66
  15.2 1.9 copy.67
  17.1 0.0 copy-done.15
  17.1 0.6 pad_maximum_fusion.2.gains.refs_3_.refs_1_
  17.7 0.1 broadcast_select_fusion.9
  17.8 19.0 %all-reduce.2 = (f32[2,8]{1,0:T(2,128)S(1)}, f32[]{:T(128)}) all-reduce(f32[2,8]{1,0:T(2,128)S(1)} %broadcast_select_fusion.9, f32[]{:T(128)S(6)} %convert_element_type.42), channel_id=1, replica_groups=mesh['section'=2,'tensor'=4,'dp'=4] {'section','dp'}, use_global_device_ids=true, to_apply=%region_4.5 | all-reduce | flops 17 | bytes 136 | tf_op jit(solution)/shard_map/psum | solution.py:598
  37.5 0.7 broadcast_multiply_fusion.1
  38.1 0.6 pad.4.router.refs_5_
  38.7 0.7 broadcast_multiply_fusion.refs_2_
  39.4 1.0 multiply_cosine_fusion
  40.4 1.0 pad_maximum_fusion.tables.refs_3_
  41.4 100.9 %forward.1 = (bf16[768,192]{1,0:T(8,128)(2,1)}, bf16[768,192]{1,0:T(8,128)(2,1)}, bf16[768,192]{1,0:T(8,128)(2,1)}, bf16[192,768]{1,0:T(8,128)(2,1)}, bf16[4,768...) custom-call(s32[2]{0:T(128)} %refs_0_.3, ...), custom_call_target="tpu_custom_call" | custom-call | tf_op jit(solution)/shard_map/forward/pallas_call | solution.py:634
  142.3 50.5 %ffn_back_1.1 = (f32[128,768]{1,0:T(8,128)}, bf16[768,3840]{1,0:T(8,128)(2,1)}, f32[1,768]{1,0:T(1,128)}, f32[8,768]{1,0:T(8,128)}) custom-call(s32[2]{0:T(128)} %refs_0_.3, bf16[128,768]{1,0:T(8,128)(2,1)} %get-tuple-element.60.refs_1_, f32[2,8,512]{2,1,0:T(8,128)} %broadcast_multiply_fusion.refs_2_, f32[2,768]{1,0:T(2,128)} %pad_maximum_fusion.2.gains.refs_3_.refs_1_, ...), custom_call_target="tpu_custom_call" | custom-call | tf_op jit(solution)/shard_map/ffn_back_1/pallas_call | solution.py:688
  192.8 0.0 reduce-scatter.11.cloned.1.call-update
  192.9 0.0 reduce-scatter.9.cloned.1.call-start
  192.9 30.5 %attn_back_1.1 = (bf16[128,768]{1,0:T(8,128)(2,1)}, f32[2,128,768]{2,1,0:T(8,128)}, bf16[2,768,192]{2,1,0:T(8,128)(2,1)}, f32[1,768]{1,0:T(1,128)}) custom-call(f32[128,768]{1,0:T(8,128)} %get-tuple-element.75.refs_0_, f32[2,768]{1,0:T(2,128)} %pad_maximum_fusion.2.gains.refs_3_.refs_1_, f32[2,768]{1,0:T(2,128)} %get-tuple-element.61.refs_4_.refs_2_, ...), custom_call_target="tpu_custom_call" | custom-call | tf_op jit(solution)/shard_map/attn_back_1/pallas_call | solution.py:728
  223.4 47.0 %ffn_back_0.1 = (f32[128,768]{1,0:T(8,128)}, bf16[768,3840]{1,0:T(8,128)(2,1)}, f32[1,768]{1,0:T(1,128)}, f32[8,768]{1,0:T(8,128)}) custom-call(s32[2]{0:T(128)} %refs_0_.3, bf16[128,768]{1,0:T(8,128)(2,1)} %get-tuple-element.87.refs_1_, f32[2,8,512]{2,1,0:T(8,128)} %broadcast_multiply_fusion.refs_2_, f32[2,768]{1,0:T(2,128)} %pad_maximum_fusion.2.gains.refs_3_.refs_1_, ...), custom_call_target="tpu_custom_call" | custom-call | tf_op jit(solution)/shard_map/ffn_back_0/pallas_call | solution.py:688
  270.4 0.0 reduce-scatter.9.cloned.1.call-update
  270.4 0.3 reduce-scatter.5.cloned.1.call-start
  270.8 29.6 %attn_back_0.1 = (bf16[128,768]{1,0:T(8,128)(2,1)}, f32[2,128,768]{2,1,0:T(8,128)}, bf16[2,768,192]{2,1,0:T(8,128)(2,1)}, f32[1,768]{1,0:T(1,128)}) custom-call(f32[128,768]{1,0:T(8,128)} %get-tuple-element.88.refs_0_, f32[2,768]{1,0:T(2,128)} %pad_maximum_fusion.2.gains.refs_3_.refs_1_, f32[2,768]{1,0:T(2,128)} %get-tuple-element.61.refs_4_.refs_2_, ...), custom_call_target="tpu_custom_call" | custom-call | tf_op jit(solution)/shard_map/attn_back_0/pallas_call | solution.py:728
  300.4 0.0 reduce-scatter.5.cloned.1.call-update
  300.4 0.0 reduce-scatter.7.cloned.1.call-start
  300.5 0.5 reduce-scatter.7.cloned.1.call-update
  301.0 0.1 multiply_reduce_fusion
  301.1 0.7 maximum_bitcast_fusion
  301.9 46.0 %all-reduce.1 = (f32[2,10,768]{2,1,0:T(8,128)S(1)}, f32[2,8]{1,0:T(2,128)S(1)}) all-reduce(f32[2,10,768]{2,1,0:T(8,128)S(1)} %pad_maximum_fusion.1, f32[2,8]{1,0:T(2,128)S(1)} %multiply_reduce_fusion), channel_id=1, replica_groups=mesh['section'=2,'tensor'=4,'dp'=4] {'section','tensor','dp'}, use_global_device_ids=true, to_apply=%region_5.6 | all-reduce | flops 15376 | bytes 123008 | tf_op jit(solution)/shard_map/psum | solution.py:781
  347.9 0.6 fusion.3
  349.2 0.0 reduce-scatter.11.cloned.1.call-done
  349.3 53.3 %reduce-scatter.9.cloned.1.call-done = bf16[192,3840]{1,0:T(8,128)(2,1)} async-done(((bf16[768,3840]{1,0:T(8,128)(2,1)}), bf16[192,3840]{1,0:T(8,128)(2,1)}) %reduce-scatter.9.cloned.1.call-update) | async-done | bytes 1474576 | tf_op jit(solution)/shard_map/reduce_scatter | solution.py:769
  402.6 2.6 broadcast_select_fusion.2
  405.2 0.0 collective-permute-start.1
  405.2 0.6 slice_bitcast_fusion.4
  405.8 1.0 select_bitcast_fusion
  406.8 21.9 %reduce-scatter.5.cloned.1.call-done = bf16[2,192,192]{2,1,0:T(8,128)(2,1)} async-done(((bf16[2,768,192]{2,1,0:T(8,128)(2,1)}), bf16[2,192,192]{2,1,0:T(8,128)(2,1)}) %reduce-scatter.5.cloned.1.call-update) | async-done | bytes 147472 | tf_op jit(solution)/shard_map/reduce_scatter | solution.py:769
  428.8 24.8 %reduce-scatter.7.cloned.1.call-done = bf16[2,192,192]{2,1,0:T(8,128)(2,1)} async-done(((bf16[2,768,192]{2,1,0:T(8,128)(2,1)}), bf16[2,192,192]{2,1,0:T(8,128)(2,1)}) %reduce-scatter.7.cloned.1.call-update) | async-done | bytes 147472 | tf_op jit(solution)/shard_map/reduce_scatter | solution.py:769
  453.5 1.0 broadcast_select_fusion.4
  454.5 0.1 collective-permute-start
  454.6 0.6 slice_bitcast_fusion.5
  455.1 0.8 collective-permute-done
  456.0 1.0 select_convert_fusion
  457.0 0.8 slice_bitcast_fusion.3
  457.8 0.8 copy.70
  458.6 0.0 collective-permute-done.1
  458.6 3.2 broadcast_select_fusion.1
  461.8 2.7 copy.68
  464.5 2.2 copy.69
  466.8 1.3 convert_bitcast_fusion
  468.1 0.4 copy-done
  468.5 3.9 maximum_convert_fusion
  472.4 0.9 copy.76
  473.3 0.9 copy.75
  474.3 0.9 copy.74
  475.2 5.4 %slice_bitcast_fusion = (f32[1,4,512,192]{3,2,1,0:T(8,128)}, f32[1,4,192,512]{2,3,1,0:T(8,128)}, f32[1,4,192,512]{2,3,1,0:T(8,128)S(1)}) fusion(f32[192,3,5,512]{0,3,2,1:T(8,128)} %maximum_convert_fusion), kind=kLoop, calls=%fused_computation.1 | loop fusion | bytes 9437184 | tf_op jit(solution)/shard_map/broadcast_in_dim | solution.py:825
  480.6 2.8 copy.73
  483.3 2.8 copy.72
  486.1 1.7 copy.71
  487.8 0.7 copy.78
  (37 shorter events, 0.1 us)
Async XLA Ops:
  7.2 9.9 %copy-start.14 = (f32[1,768]{1,0:T(1,128)S(1)}, f32[1,768]{1,0:T(1,128)}, u32[]{:S(2)}) copy-start(f32[1,768]{1,0:T(1,128)} %param.24) | copy-start | bytes 9220
  7.2 9.9 %copy-start.15 = (f32[1,768]{1,0:T(1,128)S(1)}, f32[1,768]{1,0:T(1,128)}, u32[]{:S(2)}) copy-start(f32[1,768]{1,0:T(1,128)} %param.19) | copy-start | bytes 9220
  7.2 30.9 %copy-start.10 = (bf16[1,768,4]{1,2,0:T(4,128)(2,1)S(1)}, bf16[1,768,4]{1,2,0:T(4,128)(2,1)}, u32[]{:S(2)}) copy-start(bf16[1,768,4]{1,2,0:T(4,128)(2,1)} %param.25) | copy-start | bytes 18436
  7.2 342.0 %reduce-scatter.11.cloned.1.call-start = ((), (), s32[]{:S(2)}) async-start(), calls=%async_computation.7 | async-start | bytes 7372800 | tf_op jit(solution)/shard_map/reduce_scatter | solution.py:769
  192.9 209.7 %reduce-scatter.9.cloned.1.call-start = ((), (), s32[]{:S(2)}) async-start(), calls=%async_computation.6 | async-start | bytes 7372800 | tf_op jit(solution)/shard_map/reduce_scatter | solution.py:769
  270.4 158.3 %reduce-scatter.5.cloned.1.call-start = ((), (), s32[]{:S(2)}) async-start(), calls=%async_computation.4 | async-start | bytes 983040 | tf_op jit(solution)/shard_map/reduce_scatter | solution.py:769
  270.7 30.3 %copy-start.9 = (f32[2,8,128]{2,1,0:T(8,128)S(1)}, f32[2,8,128]{2,1,0:T(8,128)}, u32[]{:S(2)}) copy-start(f32[2,8,128]{2,1,0:T(8,128)} %get-tuple-element.101) | copy-start | bytes 24580
  270.8 30.4 %copy-start.8 = (f32[8,768]{1,0:T(8,128)S(1)}, f32[8,768]{1,0:T(8,128)}, u32[]{:S(2)}) copy-start(f32[8,768]{1,0:T(8,128)} %get-tuple-element.93) | copy-start | bytes 73732
  270.8 30.4 %copy-start.13 = (f32[1,768]{1,0:T(1,128)S(1)}, f32[1,768]{1,0:T(1,128)}, u32[]{:S(2)}) copy-start(f32[1,768]{1,0:T(1,128)} %get-tuple-element.92) | copy-start | bytes 9220
  270.8 31.0 %copy-start.7 = (f32[8,768]{1,0:T(8,128)S(1)}, f32[8,768]{1,0:T(8,128)}, u32[]{:S(2)}) copy-start(f32[8,768]{1,0:T(8,128)} %get-tuple-element.96) | copy-start | bytes 73732
  270.8 31.0 %copy-start.11 = (f32[1,768]{1,0:T(1,128)S(1)}, f32[1,768]{1,0:T(1,128)}, u32[]{:S(2)}) copy-start(f32[1,768]{1,0:T(1,128)} %get-tuple-element.95) | copy-start | bytes 9220
  270.8 31.0 %copy-start.12 = (f32[1,768]{1,0:T(1,128)S(1)}, f32[1,768]{1,0:T(1,128)}, u32[]{:S(2)}) copy-start(f32[1,768]{1,0:T(1,128)} %get-tuple-element.94) | copy-start | bytes 9220
  300.4 153.1 %reduce-scatter.7.cloned.1.call-start = ((), (), s32[]{:S(2)}) async-start(), calls=%async_computation.5 | async-start | bytes 983040 | tf_op jit(solution)/shard_map/reduce_scatter | solution.py:769
  349.2 56.6 %copy-start.4 = (f32[2,128,768]{2,1,0:T(8,128)S(1)}, f32[2,128,768]{2,1,0:T(8,128)}, u32[]{:S(2)}) copy-start(f32[2,128,768]{2,1,0:T(8,128)} %get-tuple-element.90) | copy-start | bytes 2359300
  349.2 56.6 %copy-start.5 = (f32[2,128,768]{2,1,0:T(8,128)S(1)}, f32[2,128,768]{2,1,0:T(8,128)}, u32[]{:S(2)}) copy-start(f32[2,128,768]{2,1,0:T(8,128)} %get-tuple-element.89) | copy-start | bytes 2359300
  405.2 53.4 %collective-permute-start.1 = (bf16[192,3840]{1,0:T(8,128)(2,1)}, bf16[192,3840]{1,0:T(8,128)(2,1)}, u32[]{:S(2)}, u32[]{:S(2)}) collective-permute-start(bf16[192,3840]{1,0:T(8,128)(2,1)} %broadcast_select_fusion.2), channel_id=1, source_target_pairs={{0,16},{16,0},{1,17},{17,1},{2,18},{18,2},{3,19},{19,3},{4,20},{20... | collective-permute-start | bytes 4423688 | tf_op jit(solution)/shard_map/ppermute | solution.py:798
  406.8 51.8 %copy-start.1 = (bf16[192,3840]{1,0:T(8,128)(2,1)S(1)}, bf16[192,3840]{1,0:T(8,128)(2,1)}, u32[]{:S(2)}) copy-start(bf16[192,3840]{1,0:T(8,128)(2,1)} %reduce-scatter.11.cloned.1.call-done) | copy-start | bytes 4423684
  406.8 51.8 %copy-start.2 = (bf16[192,3840]{1,0:T(8,128)(2,1)S(1)}, bf16[192,3840]{1,0:T(8,128)(2,1)}, u32[]{:S(2)}) copy-start(bf16[192,3840]{1,0:T(8,128)(2,1)} %reduce-scatter.9.cloned.1.call-done) | copy-start | bytes 4423684
  454.5 1.5 collective-permute-start
  461.8 2.7 copy-start.3
  466.8 1.7 copy-start
  486.1 1.7 copy-start.6
Sparse Core Ops, SparseCore 0:
  193.0 101.2 reduce-scatter.10
  296.6 105.9 reduce-scatter.8
  404.9 23.8 reduce-scatter.4
  430.9 22.5 reduce-scatter.6
where the time goes:
time: 505 us; the launch traced here: 497 us
  Pallas kernels  259 us (51%)
  waiting for transfers between devices  101 us (20%)
  blocking collectives  65 us (13%)
  local copies, waits for them, and re-layouts  30.5 us (6%)
  other arithmetic  22.9 us (5%)
  between operations  17.7 us (4%)
    pallas_call x1, Pallas kernels, on_device(): pl.pallas_call(functools.partial(forward_kernel, ranks), out_shape=[shape...  101 us
    reduce_scatter x4, waiting for transfers between devices, over_dp(): return lax.psum_scatter(array, 'dp', scatter_dimension=dim, tiled=True)  100 us
    pallas_call x2, Pallas kernels, ffn_back(): pl.pallas_call(functools.partial(ffn_back_kernel, l, ranks), out_shape=[s...  97.5 us
    pallas_call x2, Pallas kernels, attn_back(): pl.pallas_call(functools.partial(attn_back_kernel, l, ranks), out_shape=[...  60.1 us
    psum x1, blocking collectives, on_device(): lax.psum(jnp.stack([jnp.concatenate([attn_gain_0, ffn_gain_0, router_0],...  46 us
    psum x1, blocking collectives, on_device(): lax.psum((counts_placed, jnp.sum(lengths).astype(f32)), ('section', 'dp'))  19 us
    unnamed x43, local copies, waits for them, and re-layouts  17.6 us
  transfers between devices with their start and end apart: 6, of which 4 were waited for; matrix products, arithmetic and copies ran while one was open for 2% of the time, Pallas kernels for 22%

commit v1 on v0

v1 whole, which is shorter than its diff:
```python
import functools

import jax
import jax.numpy as jnp
import numpy as np
from jax import lax
from jax.experimental import pallas as pl
from jax.experimental.pallas import tpu as pltpu
from jax.sharding import PartitionSpec as P

HEAD_DIM = 64
HALF_DIM = HEAD_DIM // 2
EPSILON = 1e-06
ALPHA = 0.01
THETA = 10000.0
MASKED = -1e30
LANES = 256
VMEM_LIMIT = 63 * 2**20

f32 = jnp.float32
bf16 = jnp.bfloat16
MESH = pl.DeviceIdType.MESH
ANY = pl.BlockSpec(memory_space=pl.ANY)
VMEM = pl.BlockSpec(memory_space=pltpu.VMEM)
SMEM = pl.BlockSpec(memory_space=pltpu.SMEM)


def dot(left, right, left_dim, right_dim):
    return lax.dot_general(
        left, right, (((left_dim,), (right_dim,)), ((), ())), preferred_element_type=f32
    )


def rope_tables(seq_len):
    frequency = (THETA ** (-np.arange(HALF_DIM, dtype=np.float32) / HALF_DIM)).astype(np.float32)
    angles = np.arange(seq_len, dtype=np.float32)[:, None] * frequency[None, :]
    cosine, sine = np.cos(angles), np.sin(angles)
    return np.concatenate([cosine, cosine, -sine, sine], axis=-1).astype(np.float32)


def turn_halves(values):
    return jnp.concatenate([values[:, HALF_DIM:], values[:, :HALF_DIM]], axis=1)


class Place:
    def __init__(self, ranks, planes):
        self.s = lax.axis_index("section")
        self.t = lax.axis_index("tensor")
        self.z = lax.axis_index("dp")
        self.ranks, self.planes = ranks, planes
        self.odd = lax.rem(self.z, 2)
        self.sibling = (1 - self.s, self.t, self.z)
        self.partner = (self.s, self.t, self.z + 1 - 2 * self.odd)

    def peer(self, k):
        return lax.rem(self.t + k, self.ranks)

    def peer_id(self, k):
        return (self.s, self.peer(k), self.z)

    def plane_id(self, k):
        return (self.s, self.t, lax.rem(self.z + k, self.planes))

    def greet(self, both_cores):
        barrier = pltpu.get_barrier_semaphore()
        others = [self.sibling] + [self.peer_id(k) for k in range(1, self.ranks)]
        for k in range(1, self.planes):
            _, t, z = self.plane_id(k)
            others += [(self.s, t, z)] + ([(1 - self.s, t, z)] if both_cores else [])
        for other in others:
            pl.semaphore_signal(barrier, inc=1, device_id=other, device_id_type=MESH)
        pl.semaphore_wait(barrier, len(others))


def remote(src, dst, send, recv, device):
    return pltpu.make_async_remote_copy(
        src_ref=src, dst_ref=dst, send_sem=send, recv_sem=recv, device_id=device, device_id_type=MESH
    )


def gather_rows(place, full, rows, send, recv):
    mine = full.at[pl.ds(place.t * rows, rows)]
    copies = []
    for k in range(1, place.ranks):
        copy = remote(mine, mine, send.at[k - 1], recv.at[k - 1], place.peer_id(k))
        copy.start()
        copies.append(copy)
    return copies


def scatter_block(place, stage, landing, rows, lo, width, send, recv):
    copies = []
    for k in range(1, place.ranks):
        src = stage.at[pl.ds(place.peer(k) * rows, rows), pl.ds(lo, width)]
        dst = landing.at[k - 1, :, pl.ds(lo, width)]
        copy = remote(src, dst, send.at[k - 1], recv.at[k - 1], place.peer_id(k))
        copy.start()
        copies.append(copy)
    return copies


def landed_sum(own, landing, ranks):
    total = own
    for k in range(ranks - 1):
        total = total + landing[k].astype(f32)
    return total


def rms_rows(values, gain):
    return values * lax.rsqrt(jnp.mean(values * values, axis=-1, keepdims=True) + EPSILON) * gain


def rms_back(values, gain, grad):
    r = lax.rsqrt(jnp.mean(values * values, axis=-1, keepdims=True) + EPSILON)
    normed = values * r
    scaled = grad * gain
    inner = jnp.mean(scaled * normed, axis=-1, keepdims=True)
    return r * (scaled - normed * inner), jnp.sum(grad * normed, axis=0, keepdims=True)


def name_rows(routes):
    expert = lax.broadcasted_iota(jnp.int32, (8, routes.shape[1]), 0)
    named = routes[0:1] == expert
    for j in range(1, routes.shape[0]):
        named = named | (routes[j : j + 1] == expert)
    return named.astype(f32)


def column(matrix, index):
    lane = lax.broadcasted_iota(jnp.int32, matrix.shape, 1)
    return jnp.sum(jnp.where(lane == index, matrix, 0.0), axis=1, keepdims=True)


def load_choice(first, pairs, sems):
    for i, (own, other, dst) in enumerate(pairs):

        @pl.when(first)
        def _(own=own, dst=dst, i=i):
            pltpu.make_async_copy(own, dst, sems.at[i]).start()

        @pl.when(jnp.logical_not(first))
        def _(other=other, dst=dst, i=i):
            pltpu.make_async_copy(other, dst, sems.at[i]).start()

    return [pltpu.make_async_copy(own, dst, sems.at[i]) for i, (own, other, dst) in enumerate(pairs)]


N_ATTN = 4
N_FFN = 6
N_STATE = 9


def attn_targets(w_in, w_out, heads_width):
    return [w_in.at[pl.ds(i * heads_width, heads_width)] for i in range(3)] + [w_out]


def ffn_targets(wg, wu, wd):
    experts = wg.shape[0] - 1
    first = pl.ds(0, experts)
    return [wg.at[first], wu.at[first], wd.at[first], wg.at[experts], wu.at[experts], wd.at[experts]]


def forward_kernel(ranks, planes, lens, bnd, routes, gain_a_own, gain_f_own, router, tables, *refs):
    own, refs = refs[:10], refs[10:]
    other, refs = refs[:10], refs[10:]
    (o_gain_a, o_gain_f, o_router, out_rows, cot, probs_sum, cnt, o_cnt), refs = refs[:8], refs[8:]
    (nf_o, q_o, k_o, v_o, p_o, mx_o, hf_o, g_o, u_o, hp_o), refs = refs[:10], refs[10:]
    (xs, mid, small, o_small), refs = refs[:4], refs[4:]
    (nf, qs, ks, vs, ps, mx, hf, gs, us), refs = refs[:9], refs[9:]
    (w_in, wo, wg, wu, wd, acts, stage, land_a, land_f, tmp, own_part), refs = refs[:11], refs[11:]
    (o_bnd, o_routes, y_low, coef, cnt_in), refs = refs[:5], refs[5:]
    (ag_s, ag_r, rsa_s, rsa_r, rsf_s, rsf_r, ex_s, ex_r, load_sem, save_sem, row_s, row_r), refs = (
        refs[:12],
        refs[12:],
    )
    (hp_s, hp_r, cz_s, cz_r, cs_s, cs_r) = refs

    place = Place(ranks, planes)
    s, t = place.s, place.t
    rows, width = bnd.shape[1], bnd.shape[2]
    seq_len = nf.shape[1]
    experts = wg.shape[0] - 1
    heads = qs.shape[1]
    heads_width = heads * HEAD_DIM
    mine = pl.ds(t * rows, rows)
    place.greet(False)

    ex_pairs = [
        (bnd.at[1 - s], o_bnd),
        (gain_a_own, o_gain_a),
        (gain_f_own, o_gain_f),
        (router, o_router),
        (routes.at[1 - s], o_routes),
    ] + [(own[i], other[i]) for i in range(10)]
    exchange = [
        remote(src, dst, ex_s.at[i], ex_r.at[i], place.sibling) for i, (src, dst) in enumerate(ex_pairs)
    ]
    for copy in exchange:
        copy.start()
    first_w = 5
    here_tokens = lax.broadcasted_iota(jnp.int32, (8, seq_len), 1)
    counted = jnp.zeros((8, 1), f32)
    for q in range(2):
        live = jnp.where(here_tokens < lens[q], 1.0, 0.0)
        row8 = lax.broadcasted_iota(jnp.int32, (8, seq_len), 0)
        counts = jnp.where(row8 == 7, live, name_rows(routes[q]) * live)
        counted = counted + jnp.sum(counts, axis=1, keepdims=True)
    cnt[...] = jnp.broadcast_to(counted, cnt.shape)
    count_copies = []
    for k in range(1, planes):
        copy = remote(cnt, cnt_in.at[k - 1], cz_s.at[k - 1], cz_r.at[k - 1], place.plane_id(k))
        copy.start()
        count_copies.append(copy)
    for copy in exchange[:first_w]:
        copy.wait()
    is_first = s == 0
    xs[0] = jnp.where(is_first, bnd[0], o_bnd[...])
    xs[1] = jnp.zeros_like(xs[1])
    cot[...] = jnp.where(is_first, o_bnd[...], bnd[1])
    length = lens[s]

    def layer(l, carry):
        here = s == l
        gain_a = jnp.where(here, gain_a_own[...], o_gain_a[...])
        gain_f = jnp.where(here, gain_f_own[...], o_gain_f[...])
        x = xs[l].astype(f32)
        nf[l, mine] = rms_rows(x, gain_a).astype(bf16)
        ag = gather_rows(place, nf.at[l], rows, ag_s.at[l, 0], ag_r.at[l, 0])

        @pl.when(jnp.logical_not(here))
        def _():
            for copy in exchange[first_w : first_w + N_ATTN]:
                copy.wait_recv()

        attn_dst = attn_targets(w_in, wo, heads_width)
        loads = load_choice(here, [(own[i], other[i], attn_dst[i]) for i in range(N_ATTN)], load_sem)

        @pl.when(jnp.logical_not(here))
        def _():
            for copy in exchange[first_w + N_ATTN :]:
                copy.wait_recv()

        ffn_dst = ffn_targets(wg, wu, wd)
        ffn_loads = load_choice(
            here,
            [(own[4 + i], other[4 + i], ffn_dst[i]) for i in range(N_FFN)],
            load_sem.at[pl.ds(N_ATTN, N_FFN)],
        )
        for copy in loads:
            copy.wait()
        for copy in ag:
            copy.wait()
        pltpu.make_async_copy(nf.at[l], nf_o.at[l], save_sem.at[l, 0]).start()
        cosine, signed = tables[:, :HEAD_DIM], tables[:, HEAD_DIM:]
        projected = dot(nf[l], w_in[...], 1, 1)
        for j, dst in enumerate((qs, ks, vs)):
            for h in range(heads):
                at = j * heads_width + h * HEAD_DIM
                piece = projected[:, at : at + HEAD_DIM]
                if j < 2:
                    piece = piece * cosine + turn_halves(piece) * signed
                dst[l, h] = piece.astype(bf16)
        for i in range(ranks):
            lo, reach = i * rows, (i + 1) * rows
            place_q = lax.broadcasted_iota(jnp.int32, (rows, reach), 0) + lo
            place_k = lax.broadcasted_iota(jnp.int32, (rows, reach), 1)
            allowed = (place_k <= place_q) & (place_k < length)
            for h in range(heads):
                scores = dot(qs[l, h, lo:reach], ks[l, h, 0:reach], 1, 1) * HEAD_DIM ** (-0.5)
                scores = jnp.where(allowed, scores, MASKED)
                peak = jnp.max(scores, axis=-1, keepdims=True)
                raised = jnp.exp(scores - peak)
                total = jnp.sum(raised, axis=-1, keepdims=True)
                weights = (raised / total).astype(bf16)
                ps[l, h, lo:reach, 0:reach] = weights
                if reach < seq_len:
                    ps[l, h, lo:reach, reach:] = jnp.zeros((rows, seq_len - reach), bf16)
                mixed = dot(weights, vs[l, h, 0:reach], 1, 0)
                mx[l, lo:reach, h * HEAD_DIM : (h + 1) * HEAD_DIM] = mixed.astype(bf16)
            part = dot(mx[l, lo:reach], wo[...], 1, 0)
            stage[lo:reach] = part.astype(bf16)

            @pl.when(t == i)
            def _(part=part):
                own_part[...] = part

            @pl.when(t != i)
            def _(i=i, lo=lo):
                k = lax.rem(i - t + ranks, ranks)
                remote(
                    stage.at[pl.ds(lo, rows)],
                    land_a.at[l, k - 1],
                    rsa_s.at[l, k - 1],
                    rsa_r.at[l, k - 1],
                    (s, i, place.z),
                ).start()

        saves = [(qs, q_o), (ks, k_o), (vs, v_o), (ps, p_o), (mx, mx_o)]
        for i, (src, dst) in enumerate(saves):
            pltpu.make_async_copy(src.at[l], dst.at[l], save_sem.at[l, 1 + i]).start()

        @pl.when(l == 1)
        def _():
            for copy in count_copies:
                copy.wait()
            total = cnt[...]
            for k in range(planes - 1):
                total = total + cnt_in[k]
            cnt[...] = total
            remote(cnt, o_cnt, cs_s, cs_r, place.sibling).start()

        for k in range(1, ranks):
            remote(
                stage.at[pl.ds(place.peer(k) * rows, rows)],
                land_a.at[l, k - 1],
                rsa_s.at[l, k - 1],
                rsa_r.at[l, k - 1],
                place.peer_id(k),
            ).wait()
        middle = x + landed_sum(own_part[...], land_a.at[l], ranks)
        mid[l] = middle
        hf[l, mine] = rms_rows(middle, gain_f).astype(bf16)
        ag = gather_rows(place, hf.at[l], rows, ag_s.at[l, 1], ag_r.at[l, 1])
        for copy in ffn_loads:
            copy.wait()
        for copy in ag:
            copy.wait()
        pltpu.make_async_copy(hf.at[l], hf_o.at[l], save_sem.at[l, 6]).start()
        remote(hf.at[l], hp_o.at[l], hp_s.at[l, 0], hp_r.at[l, 0], place.partner).start()
        hidden = hf[l]
        route_w = jnp.where(here, router[...], o_router[...])
        names = name_rows(jnp.where(here, routes[s], o_routes[...]))
        logits = dot(route_w, hidden, 1, 1)
        expert_row = lax.broadcasted_iota(jnp.int32, logits.shape, 0)
        logits = jnp.where(expert_row < experts, logits, MASKED)
        raised = jnp.exp(logits - jnp.max(logits, axis=0, keepdims=True))
        raised = jnp.where(expert_row < experts, raised, 0.0)
        chances = raised / jnp.sum(raised, axis=0, keepdims=True)
        per_chosen = names / jnp.sum(chances * names, axis=0, keepdims=True)
        gates = chances * per_chosen
        small[l, 0:8] = chances
        small[l, 8:16] = gates
        small[l, 16:24] = per_chosen
        remote(small.at[l], o_small.at[l], hp_s.at[l, 1], hp_r.at[l, 1], place.partner).start()
        token = lax.broadcasted_iota(jnp.int32, logits.shape, 1)
        summed = jnp.sum(jnp.where(token < length, chances, 0.0), axis=1, keepdims=True)
        probs_sum[l] = jnp.broadcast_to(summed, (8, 128))
        coef[...] = jnp.where(expert_row == experts, 1.0, gates).T

        def one_expert(e, carry):
            gate_h = dot(hf[l], wg[e], 1, 0)
            up_h = dot(hf[l], wu[e], 1, 0)
            gs[l, e] = gate_h.astype(bf16)
            us[l, e] = up_h.astype(bf16)
            weight = column(coef[...], e)
            acts[e] = (gate_h * jax.nn.sigmoid(gate_h) * up_h * weight).astype(bf16)
            return carry

        lax.fori_loop(0, experts + 1, one_expert, 0)
        pltpu.make_async_copy(gs.at[l], g_o.at[l], save_sem.at[l, 7]).start()
        pltpu.make_async_copy(us.at[l], u_o.at[l], save_sem.at[l, 8]).start()
        scat = []
        for n in range(width // LANES):
            lanes = slice(n * LANES, (n + 1) * LANES)
            total = dot(acts[0], wd[0, :, lanes], 1, 0)
            for e in range(1, experts + 1):
                total = total + dot(acts[e], wd[e, :, lanes], 1, 0)
            tmp[...] = total
            stage[:, lanes] = total.astype(bf16)
            own_part[:, lanes] = tmp[mine]
            scat += scatter_block(
                place, stage, land_f.at[l], rows, n * LANES, LANES, rsf_s.at[l, n], rsf_r.at[l, n]
            )
        for copy in scat:
            copy.wait()
        output = mid[l] + landed_sum(own_part[...], land_f.at[l], ranks)
        y_low[l] = output.astype(bf16)
        xs[1] = jnp.where(l == 0, y_low[l], xs[1])

        @pl.when(here)
        def _():
            out_rows[s] = y_low[l]

        @pl.when(jnp.logical_not(here))
        def _():
            remote(y_low.at[l], out_rows.at[s], row_s, row_r, place.sibling).start()

        return carry

    lax.fori_loop(0, 2, layer, 0)
    remote(y_low.at[1 - s], out_rows.at[s], row_s, row_r, place.sibling).wait_send()
    remote(y_low.at[1 - s], out_rows.at[1 - s], row_s, row_r, place.sibling).wait_recv()
    remote(cnt, o_cnt, cs_s, cs_r, place.sibling).wait()
    for copy in exchange[first_w:]:
        copy.wait_send()
    pairs = [(nf, nf_o), (qs, q_o), (ks, k_o), (vs, v_o), (ps, p_o), (mx, mx_o), (hf, hf_o), (gs, g_o), (us, u_o)]
    for l in range(2):
        remote(hf.at[l], hp_o.at[l], hp_s.at[l, 0], hp_r.at[l, 0], place.partner).wait()
        remote(small.at[l], o_small.at[l], hp_s.at[l, 1], hp_r.at[l, 1], place.partner).wait()
        for i, (src, dst) in enumerate(pairs):
            pltpu.make_async_copy(src.at[l], dst.at[l], save_sem.at[l, i]).wait()


def back_kernel(ranks, planes, top, *refs):
    (lens, cot, gain_a_own, o_gain_a, gain_f_own, o_gain_f, router, o_router, tables), refs = refs[:9], refs[9:]
    (xs, mid, small, small_p, probs_sum, cnt, o_cnt), refs = refs[:7], refs[7:]
    (nf_i, q_i, k_i, v_i, p_i, mx_i, hf_i, g_i, u_i, hp_i), refs = refs[:10], refs[10:]
    own, refs = refs[:10], refs[10:]
    other, refs = refs[:10], refs[10:]
    (in_grads, wq_out, wk_out, wv_out, wo_out, gain_a_out, gain_f_out, router_out, balance), refs = (
        refs[:9],
        refs[9:],
    )
    ffn_outs, refs = refs[:6], refs[6:]
    (hf, gs, us, hp, wg, wu, wd), refs = refs[:7], refs[7:]
    (nf, qs, ks, vs, ps, mx, w_in, wo), refs = refs[:8], refs[8:]
    (dyf, dyp, acts, gp, up, ap, coef, coef_p, gate_sum), refs = refs[:9], refs[9:]
    (stage, land_f, land_a, tmp, own_part, d_mid), refs = refs[:6], refs[6:]
    (sent, got, quarter, land, df, ds, dqkv), refs = refs[:7], refs[7:]
    (gw, got_a, half_a, land_z, row_buf, packs, pack_t, pack_z, steps), refs = refs[:9], refs[9:]
    (ag_s, ag_r, rs_s, rs_r, agd_s, agd_r, rsd_s, rsd_r, dp_s, dp_r, ex_s, ex_r), refs = refs[:12], refs[12:]
    (zs, zr, zl, as_s, as_r, az_s, az_r, az_l, row_s, row_r, pk_s, pk_r), refs = refs[:12], refs[12:]
    (pt_s, pt_r, pz_s, pz_r, ffn_sem, attn_sem, step_sem) = refs

    place = Place(ranks, planes)
    s, t, z, odd = place.s, place.t, place.z, place.odd
    rows, width = cot.shape
    seq_len = hf.shape[0]
    experts = wg.shape[0] - 1
    blocks = experts + 1
    inner = wg.shape[2]
    half = inner // 2
    part = half // 2
    heads = qs.shape[0]
    heads_width = heads * HEAD_DIM
    chunk = width // planes
    mine = pl.ds(t * rows, rows)
    here_lanes = pl.ds(pl.multiple_of(odd * half, half), half)
    slot = s * planes + z
    scale = HEAD_DIM ** (-0.5)

    def ffn_loads(l):
        pairs = [(g_i, gs), (u_i, us), (hf_i, hf), (hp_i, hp)]
        state = [
            pltpu.make_async_copy(src.at[l], dst, ffn_sem.at[N_FFN + i]) for i, (src, dst) in enumerate(pairs)
        ]
        for copy in state:
            copy.start()
        targets = ffn_targets(wg, wu, wd)
        order = (2, 5, 0, 1, 3, 4)
        return state + load_choice(s == l, [(own[4 + i], other[4 + i], targets[i]) for i in order], ffn_sem)

    def attn_loads(l):
        pairs = [(nf_i, nf), (q_i, qs), (k_i, ks), (v_i, vs), (p_i, ps), (mx_i, mx)]
        state = [
            pltpu.make_async_copy(src.at[l], dst, attn_sem.at[N_ATTN + i])
            for i, (src, dst) in enumerate(pairs)
        ]
        for copy in state:
            copy.start()
        targets = attn_targets(w_in, wo, heads_width)
        return state + load_choice(s == l, [(own[i], other[i], targets[i]) for i in range(N_ATTN)], attn_sem)

    def to_owner(l, src, dst, send, recv, local):
        for c in range(planes):
            own_copy = (z == c) & (s == l)

            @pl.when(own_copy)
            def _(c=c):
                pltpu.make_async_copy(src(c), dst, local).start()

            @pl.when(jnp.logical_not(own_copy))
            def _(c=c):
                remote(src(c), dst, send.at[c], recv.at[slot], (l, t, c)).start()

    def sent_to_owner(l, whole, dst, send, recv, local):
        for c in range(planes):
            own_copy = (z == c) & (s == l)

            @pl.when(own_copy)
            def _(c=c):
                pltpu.make_async_copy(whole.at[c], dst.at[slot], local).wait()

            @pl.when(jnp.logical_not(own_copy))
            def _(c=c):
                remote(whole.at[c], dst.at[slot], send.at[c], recv.at[slot], (l, t, c)).wait_send()

    def arrived(dst, send, recv):
        for source in range(2 * planes):

            @pl.when(source != slot)
            def _(source=source):
                remote(
                    dst.at[source], dst.at[source], send.at[0], recv.at[source], place.sibling
                ).wait_recv()

    pending_ffn = ffn_loads(1)
    pending_attn = attn_loads(1)
    position = lax.broadcasted_iota(jnp.int32, (rows, width), 0) + t * rows
    dyf[mine] = jnp.where(position < lens[s], cot[...].astype(f32), 0.0).astype(bf16)
    place.greet(True)
    ag = gather_rows(place, dyf, rows, ag_s.at[1], ag_r.at[1])

    for l in (1, 0):
        here = s == l
        for copy in pending_ffn:
            copy.wait()
        expert_row = lax.broadcasted_iota(jnp.int32, (8, seq_len), 0)
        coef[...] = jnp.where(expert_row == experts, 1.0, small[l, 8:16]).T
        coef_p[...] = jnp.where(expert_row == experts, 1.0, small_p[l, 8:16]).T
        gate_sum[...] = jnp.zeros_like(gate_sum)
        for copy in ag:
            copy.wait()
        to_partner = remote(dyf, dyp.at[l], dp_s.at[l], dp_r.at[l], place.partner)
        to_partner.start()

        def one_expert(e, carry, l=l):
            raw = dot(dyf[...], wd[e], 1, 1)
            gate_h = gs[e].astype(f32)
            up_h = us[e].astype(f32)
            sig = jax.nn.sigmoid(gate_h)
            silu = gate_h * sig
            acted = silu * up_h
            inner_sum = jnp.sum(acted * raw, axis=1, keepdims=True)
            lane8 = lax.broadcasted_iota(jnp.int32, gate_sum.shape, 1)
            gate_sum[...] = jnp.where(lane8 == e, inner_sum, gate_sum[...])
            weight = column(coef[...], e)
            chosen_acts = acted * weight
            acts[e] = jnp.where(odd == 0, chosen_acts[:, :half], chosen_acts[:, half:]).astype(bf16)
            d_acted = raw * weight
            gs[e] = (d_acted * up_h * (sig + silu * (1.0 - sig))).astype(bf16)
            us[e] = (d_acted * silu).astype(bf16)
            return carry

        lax.fori_loop(0, blocks, one_expert, 0)
        chances, gates, per_chosen = small[l, 0:8], small[l, 8:16], small[l, 16:24]
        totals = jnp.where(here, cnt[...], o_cnt[...])
        tokens_all = totals[7:8, 0:1]
        share = totals[:, 0:1] / (top * tokens_all)
        token = lax.broadcasted_iota(jnp.int32, (8, seq_len), 1)
        aux = jnp.where((token < lens[s]) & (t == 0), ALPHA * experts * share / tokens_all, 0.0)
        d_gates = gate_sum[...].T
        common = jnp.sum(d_gates * gates, axis=0, keepdims=True)
        d_chances = per_chosen * (d_gates - common) + aux
        d_logits = chances * (d_chances - jnp.sum(chances * d_chances, axis=0, keepdims=True))
        d_logits = d_logits.astype(bf16)
        router_grad = dot(d_logits, hf[...], 1, 0)
        route_w = jnp.where(here, router[...], o_router[...])
        scat = []
        for n in range(width // LANES):
            lanes = slice(n * LANES, (n + 1) * LANES)
            total = dot(d_logits, route_w[:, lanes], 0, 0)
            for e in range(blocks):
                total = total + dot(gs[e], wg[e, lanes], 1, 1)
                total = total + dot(us[e], wu[e, lanes], 1, 1)
            tmp[...] = total
            stage[:, lanes] = total.astype(bf16)
            own_part[:, lanes] = tmp[mine]
            scat += scatter_block(
                place, stage, land_f, rows, n * LANES, LANES, rs_s.at[l, n], rs_r.at[l, n]
            )
        to_partner.wait()

        def partner_expert(e, carry, l=l):
            gate_h = dot(hp[...], wg[e, :, here_lanes], 1, 0)
            up_h = dot(hp[...], wu[e, :, here_lanes], 1, 0)
            raw = dot(dyp[l], wd[e, here_lanes], 1, 1)
            sig = jax.nn.sigmoid(gate_h)
            silu = gate_h * sig
            weight = column(coef_p[...], e)
            ap[e] = (silu * up_h * weight).astype(bf16)
            d_acted = raw * weight
            gp[e] = (d_acted * up_h * (sig + silu * (1.0 - sig))).astype(bf16)
            up[e] = (d_acted * silu).astype(bf16)
            return carry

        lax.fori_loop(0, blocks, partner_expert, 0)
        for copy in scat:
            copy.wait()
        d_hidden = landed_sum(own_part[...], land_f, ranks)
        gain_f = jnp.where(here, gain_f_own[...], o_gain_f[...])
        d_norm, gain_f_grad = rms_back(mid[l], gain_f, d_hidden)
        d_mid[...] = dyf[mine].astype(f32) + d_norm
        df[mine] = d_mid[...].astype(bf16)
        ag = gather_rows(place, df, rows, agd_s.at[l], agd_r.at[l])

        def swap_of(e, l=l):
            return remote(sent.at[lax.rem(e, 2)], got.at[e], ex_s.at[e], ex_r.at[e], place.sibling)

        def finish(e, l=l):
            swap_of(e).wait()
            for j in range(3):
                at = e * 3 + j
                for c in range(planes):
                    quarter[l, c, at] = (
                        quarter[l, c, at].astype(f32) + got[e, j, c].astype(f32)
                    ).astype(bf16)
            three = pl.ds(e * 3, 3)
            to_owner(
                l, lambda c: quarter.at[l, c, three], land.at[slot, three], zs.at[l], zr, zl.at[l]
            )

        def weight_grads(e, carry, l=l):
            sources = ((hf, gs, hp, gp), (hf, us, hp, up))
            for j in range(3):
                if j < 2:
                    left, right, left_p, right_p = sources[j]
                    value = dot(left[...], right[e, :, here_lanes], 0, 0) + dot(left_p[...], right_p[e], 0, 0)
                else:
                    value = dot(dyf[...], acts[e], 0, 0) + dot(dyp[l], ap[e], 0, 0)
                low, high = value[:, :part], value[:, part:]
                kept = jnp.where(s == 0, low, high).astype(bf16)
                given = jnp.where(s == 0, high, low).astype(bf16)
                for c in range(planes):
                    quarter[l, c, e * 3 + j] = kept[c * chunk : (c + 1) * chunk]
                    sent[lax.rem(e, 2), j, c] = given[c * chunk : (c + 1) * chunk]
            swap_of(e).start()

            @pl.when(e > 0)
            def _():
                finish(e - 1)

            return carry

        lax.fori_loop(0, blocks, weight_grads, 0)
        finish(blocks - 1)
        if l == 1:
            pending_ffn = ffn_loads(0)
        for copy in pending_attn:
            copy.wait()
        for copy in ag:
            copy.wait()
        cosine, signed = tables[:, :HEAD_DIM], tables[:, HEAD_DIM:]
        for h in range(heads):
            span = slice(h * HEAD_DIM, (h + 1) * HEAD_DIM)
            d_mixed = dot(df[...], wo[span], 1, 1).astype(bf16)
            for i in range(ranks):
                lo, reach = i * rows, (i + 1) * rows
                weights = ps[h, lo:reach, 0:reach].astype(f32)
                d_probs = dot(d_mixed[lo:reach], vs[h, 0:reach], 1, 1)
                total = jnp.sum(weights * d_probs, axis=-1, keepdims=True)
                ds[lo:reach, 0:reach] = (weights * (d_probs - total)).astype(bf16)
                if reach < seq_len:
                    ds[lo:reach, reach:] = jnp.zeros((rows, seq_len - reach), bf16)
            d_value = dot(ps[h], d_mixed, 0, 0)
            d_query = dot(ds[...], ks[h], 1, 0) * scale
            d_key = dot(ds[...], qs[h], 0, 0) * scale
            d_query = d_query * cosine - turn_halves(d_query) * signed
            d_key = d_key * cosine - turn_halves(d_key) * signed
            for j, value in enumerate((d_query, d_key, d_value)):
                at = j * heads_width + h * HEAD_DIM
                dqkv[:, at : at + HEAD_DIM] = value.astype(bf16)
        scat = []
        for n in range(width // LANES):
            lanes = slice(n * LANES, (n + 1) * LANES)
            total = dot(dqkv[...], w_in[:, lanes], 1, 0)
            tmp[...] = total
            stage[:, lanes] = total.astype(bf16)
            own_part[:, lanes] = tmp[mine]
            scat += scatter_block(
                place, stage, land_a, rows, n * LANES, LANES, rsd_s.at[l, n], rsd_r.at[l, n]
            )
        three_widths = 3 * heads_width
        gw[:, :three_widths] = dot(nf[...], dqkv[...], 0, 0).astype(bf16)
        gw[:, three_widths:] = dot(df[...], mx[...], 0, 0).astype(bf16)
        side = 2 * heads_width
        swap = remote(
            gw.at[:, pl.ds(pl.multiple_of((1 - s) * side, 128), side)], got_a, as_s.at[l], as_r.at[l], place.sibling
        )
        swap.start()
        for copy in scat:
            copy.wait()
        d_normed = landed_sum(own_part[...], land_a, ranks)
        gain_a = jnp.where(here, gain_a_own[...], o_gain_a[...])
        d_norm, gain_a_grad = rms_back(xs[l].astype(f32), gain_a, d_normed)
        dx = d_mid[...] + d_norm
        if l == 1:
            low_dx = dx.astype(bf16)
            dyf[mine] = low_dx
            ag = gather_rows(place, dyf, rows, ag_s.at[0], ag_r.at[0])
            dx = low_dx.astype(f32)
        swap.wait()
        kept = gw[:, pl.ds(pl.multiple_of(s * side, 128), side)].astype(f32) + got_a[...].astype(f32)
        kept = kept.astype(bf16)
        if l == 0:
            sent_to_owner(1, half_a, land_z, az_s.at[1], az_r, az_l.at[1])
        for c in range(planes):
            half_a[c] = kept[c * chunk : (c + 1) * chunk]
        to_owner(l, lambda c: half_a.at[c], land_z.at[slot], az_s.at[l], az_r, az_l.at[l])
        if l == 1:
            pending_attn = attn_loads(0)
        pack = jnp.concatenate(
            [
                jnp.concatenate([gain_a_grad, gain_f_grad, jnp.zeros((6, width), f32), router_grad], axis=0),
                jnp.concatenate(
                    [jnp.zeros((8, 128), f32), jnp.where(t == 0, probs_sum[l], 0.0)], axis=0
                ),
            ],
            axis=1,
        )

        @pl.when(here)
        def _(dx=dx, pack=pack):
            in_grads[s] = dx
            packs[0] = pack

        @pl.when(jnp.logical_not(here))
        def _(dx=dx, pack=pack):
            row_buf[...] = dx
            packs[1] = pack
            remote(row_buf, in_grads.at[s], row_s, row_r, place.sibling).start()
            remote(packs.at[1], packs.at[2], pk_s, pk_r, place.sibling).start()

    remote(packs.at[1], packs.at[2], pk_s, pk_r, place.sibling).wait()
    packs[0] = packs[0] + packs[2]
    copies = []
    for k in range(1, ranks):
        copy = remote(packs.at[0], pack_t.at[k - 1], pt_s.at[k - 1], pt_r.at[k - 1], place.peer_id(k))
        copy.start()
        copies.append(copy)
    for copy in copies:
        copy.wait()
    total = packs[0]
    for k in range(ranks - 1):
        total = total + pack_t[k]
    packs[0] = total
    copies = []
    for k in range(1, planes):
        copy = remote(packs.at[0], pack_z.at[k - 1], pz_s.at[k - 1], pz_r.at[k - 1], place.plane_id(k))
        copy.start()
        copies.append(copy)
    for copy in copies:
        copy.wait()
    total = packs[0]
    for k in range(planes - 1):
        total = total + pack_z[k]
    gain_a_out[...] = total[0:1, :width]
    gain_f_out[...] = total[1:2, :width]
    router_out[...] = total[8 : 8 + experts, :width]
    tokens_all = cnt[7:8, 0:1]
    products = cnt[0:experts, 0:1] / (top * tokens_all) * total[8 : 8 + experts, width : width + 1]
    balance[...] = experts * jnp.sum(products, axis=0, keepdims=True) / tokens_all

    remote(row_buf, in_grads.at[s], row_s, row_r, place.sibling).wait_send()
    remote(row_buf, in_grads.at[1 - s], row_s, row_r, place.sibling).wait_recv()
    for l in (1, 0):
        sent_to_owner(l, quarter.at[l], land, zs.at[l], zr, zl.at[l])
    sent_to_owner(0, half_a, land_z, az_s.at[0], az_r, az_l.at[0])
    arrived(land, zs.at[0], zr)
    pieces = []
    for e in range(blocks):
        for j in range(3):
            at = len(pieces)
            room = at % 2
            if e < experts:
                target = ffn_outs[j].at[e]
            else:
                target = ffn_outs[3 + j]
            if at >= 2:
                pieces[at - 2].wait()
            for core in range(2):
                for parity in range(2):
                    value = land[core * planes + parity, e * 3 + j].astype(f32)
                    for pair in range(1, planes // 2):
                        value = value + land[core * planes + 2 * pair + parity, e * 3 + j].astype(f32)
                    lo = (2 * parity + core) * part
                    steps[room, :, lo : lo + part] = value
            copy = pltpu.make_async_copy(steps.at[room], target, step_sem.at[room])
            copy.start()
            pieces.append(copy)
    arrived(land_z, az_s.at[0], az_r)
    sides = []
    for core in range(2):
        value = land_z[core * planes].astype(f32)
        for plane in range(1, planes):
            value = value + land_z[core * planes + plane].astype(f32)
        sides.append(value)
    wq_out[...] = sides[0][:, :heads_width]
    wk_out[...] = sides[0][:, heads_width:]
    wv_out[...] = sides[1][:, :heads_width]
    wo_out[...] = sides[1][:, heads_width:].T
    for copy in pieces[-2:]:
        copy.wait()


def params(collective_id):
    return pltpu.CompilerParams(
        collective_id=collective_id, has_side_effects=True, vmem_limit_bytes=VMEM_LIMIT
    )


def shape_of(*dims, dtype=bf16):
    return jax.ShapeDtypeStruct(dims, dtype)


def on_device(ranks, planes, *args):
    (boundary, lengths, routes, attn_gain, w_query, w_key, w_value, w_out, ffn_gain, router) = args[:10]
    ffn_own = tuple(a[0] for a in args[10:])
    attn_own = (w_query[0].T, w_key[0].T, w_value[0].T, w_out[0])
    rows, width = boundary.shape[2:]
    seqs, seq_len = routes.shape[1:3]
    top = routes.shape[3]
    experts, _, inner = ffn_own[0].shape
    blocks = experts + 1
    heads_width = w_query.shape[2]
    heads = heads_width // HEAD_DIM
    chunks = width // LANES
    half, part = inner // 2, inner // 4
    chunk = width // planes
    peers = ranks - 1
    dma = pltpu.SemaphoreType.DMA

    routes_t = jnp.swapaxes(routes[0], 1, 2)
    router_t = jnp.pad(router[0].T, ((0, 8 - experts), (0, 0)))
    tables = jnp.asarray(rope_tables(seq_len))

    states = [
        shape_of(2, seq_len, width),
        shape_of(2, heads, seq_len, HEAD_DIM),
        shape_of(2, heads, seq_len, HEAD_DIM),
        shape_of(2, heads, seq_len, HEAD_DIM),
        shape_of(2, heads, seq_len, seq_len),
        shape_of(2, seq_len, heads_width),
        shape_of(2, seq_len, width),
        shape_of(2, blocks, seq_len, inner),
        shape_of(2, blocks, seq_len, inner),
    ]
    partner_hidden = shape_of(2, seq_len, width)
    weights = attn_own + ffn_own
    ffn_scratch = [
        pltpu.VMEM((blocks, width, inner), bf16),
        pltpu.VMEM((blocks, width, inner), bf16),
        pltpu.VMEM((blocks, inner, width), bf16),
    ]
    attn_scratch = [pltpu.VMEM((3 * heads_width, width), bf16), pltpu.VMEM((heads_width, width), bf16)]
    result = pl.pallas_call(
        functools.partial(forward_kernel, ranks, planes),
        out_shape=[shape_of(*w.shape) for w in weights]
        + [
            shape_of(1, width, dtype=f32),
            shape_of(1, width, dtype=f32),
            shape_of(8, width),
            shape_of(2, rows, width),
            shape_of(rows, width),
            shape_of(2, 8, 128, dtype=f32),
            shape_of(8, 128, dtype=f32),
            shape_of(8, 128, dtype=f32),
        ]
        + states
        + [partner_hidden]
        + [
            shape_of(2, rows, width),
            shape_of(2, rows, width, dtype=f32),
            shape_of(2, 24, seq_len, dtype=f32),
            shape_of(2, 24, seq_len, dtype=f32),
        ],
        in_specs=[SMEM] + [VMEM] * 6 + [ANY] * 10,
        out_specs=[ANY] * 10 + [VMEM] * 8 + [ANY] * 10 + [VMEM] * 4,
        scratch_shapes=[pltpu.VMEM(st.shape, st.dtype) for st in states]
        + attn_scratch
        + ffn_scratch
        + [
            pltpu.VMEM((blocks, seq_len, inner), bf16),
            pltpu.VMEM((seq_len, width), bf16),
            pltpu.VMEM((2, peers, rows, width), bf16),
            pltpu.VMEM((2, peers, rows, width), bf16),
            pltpu.VMEM((seq_len, LANES), f32),
            pltpu.VMEM((rows, width), f32),
            pltpu.VMEM((rows, width), bf16),
            pltpu.VMEM((top, seq_len), jnp.int32),
            pltpu.VMEM((2, rows, width), bf16),
            pltpu.VMEM((seq_len, 8), f32),
            pltpu.VMEM((planes - 1, 8, 128), f32),
            dma((2, 2, peers)),
            dma((2, 2, peers)),
            dma((2, peers)),
            dma((2, peers)),
            dma((2, chunks, peers)),
            dma((2, chunks, peers)),
            dma((15,)),
            dma((15,)),
            dma((10,)),
            dma((2, 9)),
            dma,
            dma,
            dma((2, 2)),
            dma((2, 2)),
            dma((planes - 1,)),
            dma((planes - 1,)),
            dma,
            dma,
        ],
        compiler_params=params(0),
        name="forward",
    )(lengths, boundary[0], routes_t, attn_gain, ffn_gain, router_t, tables, *weights)
    other, result = result[:10], result[10:]
    (o_gain_a, o_gain_f, o_router, out_rows, cot, probs_sum, cnt, o_cnt), result = result[:8], result[8:]
    saved, result = result[:10], result[10:]
    (xs, mid, small, o_small) = result

    (in_grads, g_q, g_k, g_v, g_o, g_gain_a, g_gain_f, g_router, balance, *g_ffn) = pl.pallas_call(
        functools.partial(back_kernel, ranks, planes, top),
        out_shape=[shape_of(seqs, rows, width, dtype=f32)]
        + [shape_of(chunk, heads_width, dtype=f32)] * 3
        + [
            shape_of(heads_width, chunk, dtype=f32),
            shape_of(1, width, dtype=f32),
            shape_of(1, width, dtype=f32),
            shape_of(experts, width, dtype=f32),
            shape_of(1, 1, dtype=f32),
        ]
        + [shape_of(experts, chunk, inner, dtype=f32)] * 3
        + [shape_of(chunk, inner, dtype=f32)] * 3,
        in_specs=[SMEM] + [VMEM] * 15 + [ANY] * 30,
        out_specs=[VMEM] * 9 + [ANY] * 6,
        scratch_shapes=[
            pltpu.VMEM((seq_len, width), bf16),
            pltpu.VMEM((blocks, seq_len, inner), bf16),
            pltpu.VMEM((blocks, seq_len, inner), bf16),
            pltpu.VMEM((seq_len, width), bf16),
        ]
        + ffn_scratch
        + [pltpu.VMEM(st.shape[1:], st.dtype) for st in states[:6]]
        + attn_scratch
        + [
            pltpu.VMEM((seq_len, width), bf16),
            pltpu.VMEM((2, seq_len, width), bf16),
            pltpu.VMEM((blocks, seq_len, half), bf16),
            pltpu.VMEM((blocks, seq_len, half), bf16),
            pltpu.VMEM((blocks, seq_len, half), bf16),
            pltpu.VMEM((blocks, seq_len, half), bf16),
            pltpu.VMEM((seq_len, 8), f32),
            pltpu.VMEM((seq_len, 8), f32),
            pltpu.VMEM((seq_len, 8), f32),
            pltpu.VMEM((seq_len, width), bf16),
            pltpu.VMEM((peers, rows, width), bf16),
            pltpu.VMEM((peers, rows, width), bf16),
            pltpu.VMEM((seq_len, LANES), f32),
            pltpu.VMEM((rows, width), f32),
            pltpu.VMEM((rows, width), f32),
            pltpu.VMEM((2, 3, planes, chunk, part), bf16),
            pltpu.VMEM((blocks, 3, planes, chunk, part), bf16),
            pltpu.VMEM((2, planes, 3 * blocks, chunk, part), bf16),
            pltpu.VMEM((2 * planes, 3 * blocks, chunk, part), bf16),
            pltpu.VMEM((seq_len, width), bf16),
            pltpu.VMEM((seq_len, seq_len), bf16),
            pltpu.VMEM((seq_len, 3 * heads_width), bf16),
            pltpu.VMEM((width, 4 * heads_width), bf16),
            pltpu.VMEM((width, 2 * heads_width), bf16),
            pltpu.VMEM((planes, chunk, 2 * heads_width), bf16),
            pltpu.VMEM((2 * planes, chunk, 2 * heads_width), bf16),
            pltpu.VMEM((rows, width), f32),
            pltpu.VMEM((3, 16, width + 128), f32),
            pltpu.VMEM((peers, 16, width + 128), f32),
            pltpu.VMEM((planes - 1, 16, width + 128), f32),
            pltpu.VMEM((2, chunk, inner), f32),
            dma((2, peers)),
            dma((2, peers)),
            dma((2, chunks, peers)),
            dma((2, chunks, peers)),
            dma((2, peers)),
            dma((2, peers)),
            dma((2, chunks, peers)),
            dma((2, chunks, peers)),
            dma((2,)),
            dma((2,)),
            dma((blocks,)),
            dma((blocks,)),
            dma((2, planes)),
            dma((2 * planes,)),
            dma((2,)),
            dma((2,)),
            dma((2,)),
            dma((2, planes)),
            dma((2 * planes,)),
            dma((2,)),
            dma,
            dma,
            dma,
            dma,
            dma((peers,)),
            dma((peers,)),
            dma((planes - 1,)),
            dma((planes - 1,)),
            dma((10,)),
            dma((10,)),
            dma((2,)),
        ],
        compiler_params=params(1),
        name="backward",
    )(
        lengths,
        cot,
        attn_gain,
        o_gain_a,
        ffn_gain,
        o_gain_f,
        router_t,
        o_router,
        tables,
        xs,
        mid,
        small,
        o_small,
        probs_sum,
        cnt,
        o_cnt,
        *saved,
        *weights,
        *other,
    )
    g_eg, g_eu, g_ed, g_sg, g_su, g_sd = g_ffn
    return (
        out_rows[None],
        in_grads[None],
        g_gain_a,
        g_q[None],
        g_k[None],
        g_v[None],
        g_o[None],
        g_gain_f,
        g_router.T[None],
        g_eg[None],
        g_eu[None],
        jnp.swapaxes(g_ed, 1, 2)[None],
        g_sg[None],
        g_su[None],
        g_sd.T[None],
        balance.reshape(1),
    )


def solution(mesh):
    placed = (
        P("section", "dp", "tensor", None),
        P("dp"),
        P("section", "dp", None, None),
        P("section", None),
        P("section", None, "tensor"),
        P("section", None, "tensor"),
        P("section", None, "tensor"),
        P("section", "tensor", None),
        P("section", None),
        P("section", None, None),
        P("section", None, None, "tensor"),
        P("section", None, None, "tensor"),
        P("section", None, "tensor", None),
        P("section", None, "tensor"),
        P("section", None, "tensor"),
        P("section", "tensor", None),
    )
    return jax.shard_map(
        functools.partial(on_device, mesh.shape["tensor"], mesh.shape["dp"]),
        mesh=mesh,
        in_specs=placed,
        out_specs=(
            P("section", "dp", "tensor", None),
            P("section", "dp", "tensor", None),
            P("section", None),
            P("section", "dp", "tensor"),
            P("section", "dp", "tensor"),
            P("section", "dp", "tensor"),
            P("section", "tensor", "dp"),
            P("section", None),
            P("section", None, None),
            P("section", None, "dp", "tensor"),
            P("section", None, "dp", "tensor"),
            P("section", None, "tensor", "dp"),
            P("section", "dp", "tensor"),
            P("section", "dp", "tensor"),
            P("section", "tensor", "dp"),
            P("section"),
        ),
        check_vma=False,
    )
```

time: 505 us -> 351 us (0.70)
  waiting for transfers between devices: 101 us -> 0 us
  Pallas kernels: 259 us -> 325 us
  blocking collectives: 65 us -> 0 us
  other arithmetic: 22.9 us -> 0 us
  between operations: 17.7 us -> 2.87 us
  local copies, waits for them, and re-layouts: 30.5 us -> 16.9 us
    reduce_scatter x4 -> x0, waiting for transfers between devices: 100 us -> none  [over_dp(): return lax.psum_scatter(array, 'dp', scatter_dimension=dim, tiled=True)]
    pallas_call x5 -> x2, Pallas kernels: 259 us -> 325 us  [the longest x1 220 us: on_device(): pl.pallas_call(functools.partial(back_kernel, ranks, planes, top), out_sh...]
    psum x2 -> x0, blocking collectives: 65 us -> none  [the longest x1 46 us: on_device(): lax.psum(jnp.stack([jnp.concatenate([attn_gain_0, ffn_gain_0, router_0],...]
    select_n x6 -> x0, other arithmetic: 6.9 us -> none  [the longest x2 3.59 us: swap(): jnp.where(first_section, second, first)]
    broadcast_in_dim x3 -> x0, local copies, waits for them, and re-layouts: 6.81 us -> none  [the longest x1 5.39 us: on_device(): expert_down[None]]
    convert_element_type x5 -> x0, other arithmetic: 6.27 us -> none  [the longest x1 3.91 us: on_device(): merged = jnp.concatenate(shaped, axis=-1).astype(f32)]
    unnamed x43 -> x37, local copies, waits for them, and re-layouts: 17.6 us -> 15.7 us
  transfers between devices with their start and end apart: 6 -> 0, of which waited for: 4 -> 0; matrix products, arithmetic and copies ran while one was open for 2% -> 0% of each run, Pallas kernels for 22% -> 0%
where the time goes in v1:
time: 351 us; the launch traced here: 345 us
  Pallas kernels  325 us (93%)
  local copies, waits for them, and re-layouts  16.9 us (5%)
    pallas_call x1, Pallas kernels, on_device(): pl.pallas_call(functools.partial(back_kernel, ranks, planes, top), out_sh...  220 us
    pallas_call x1, Pallas kernels, on_device(): pl.pallas_call(functools.partial(forward_kernel, ranks, planes), out_shap...  105 us
    unnamed x37, local copies, waits for them, and re-layouts  15.7 us

profile of v1, /device:TPU:0, one launch (start us, length us, event | category | flops | bytes accessed | tf_op | source)
XLA Modules:
  0.0 344.6 jit_solution(4904304678949036546)
XLA Ops:
  0.6 1.3 pad.4.router.refs_6_
  1.9 105.1 %forward.1 = (bf16[192,768]{1,0:T(8,128)(2,1)}, bf16[192,768]{1,0:T(8,128)(2,1)}, bf16[192,768]{1,0:T(8,128)(2,1)}, bf16[192,768]{1,0:T(8,128)(2,1)}, bf16[4,768...) custom-call(s32[2]{0:T(128)} %refs_0_.1, ...), custom_call_target="tpu_custom_call" | custom-call | tf_op jit(solution)/shard_map/forward/pallas_call | solution.py:836
  107.0 0.0 copy-start.6
  107.1 219.7 %backward.1 = (f32[2,128,768]{2,1,0:T(8,128)}, f32[192,192]{1,0:T(8,128)}, f32[192,192]{1,0:T(8,128)}, f32[192,192]{1,0:T(8,128)}, f32[192,192]{1,0:T(8,128)}, /...) custom-call(s32[2]{0:T(128)} %refs_0_.1, ...), custom_call_target="tpu_custom_call" | custom-call | tf_op jit(solution)/shard_map/backward/pallas_call | solution.py:901
  326.8 0.0 copy-start.8
  326.8 0.0 copy-start.7
  326.8 0.0 copy-start.10
  326.8 0.0 copy-start.9
  326.8 0.0 copy-start.2
  326.8 0.0 copy-done.6
  326.8 0.7 copy.49
  327.6 0.0 copy-start.1
  327.6 2.2 copy.50
  329.8 1.2 copy.51
  331.0 1.6 copy.52
  332.6 1.6 copy.53
  334.3 0.0 copy-done.8
  334.3 0.7 copy.54
  334.9 0.0 copy-done.7
  334.9 0.7 copy.55
  335.6 0.0 copy-done.10
  335.6 0.6 copy.56
  336.2 0.0 copy-done.9
  336.2 0.6 copy.57
  336.8 0.0 copy-done.2
  336.8 0.0 copy-start
  336.8 1.1 copy.58
  337.9 0.0 copy-done.1
  337.9 0.0 copy-start.5
  337.9 0.0 copy-start.4
  338.0 1.1 copy.59
  339.1 0.0 copy-done
  339.1 0.0 copy-start.3
  339.1 1.1 copy.60
  340.2 0.0 copy-done.5
  340.2 0.7 copy.61
  341.0 0.0 copy-done.4
  341.0 0.7 copy.62
  341.7 0.0 copy-done.3
  341.7 0.7 copy.63
Async XLA Ops:
  107.0 219.8 %copy-start.6 = (bf16[2,128,768]{2,1,0:T(8,128)(2,1)S(1)}, bf16[2,128,768]{2,1,0:T(8,128)(2,1)}, u32[]{:S(2)}) copy-start(bf16[2,128,768]{2,1,0:T(8,128)(2,1)} %get-tuple-element.63) | copy-start | bytes 1179652
  326.8 7.5 %copy-start.8 = (f32[192,192]{1,0:T(8,128)S(1)}, f32[192,192]{1,0:T(8,128)}, u32[]{:S(2)}) copy-start(f32[192,192]{1,0:T(8,128)} %get-tuple-element.99) | copy-start | bytes 442372
  326.8 8.1 %copy-start.7 = (f32[192,192]{1,0:T(8,128)S(1)}, f32[192,192]{1,0:T(8,128)}, u32[]{:S(2)}) copy-start(f32[192,192]{1,0:T(8,128)} %get-tuple-element.100) | copy-start | bytes 442372
  326.8 8.8 %copy-start.10 = (f32[1,768]{1,0:T(1,128)S(1)}, f32[1,768]{1,0:T(1,128)}, u32[]{:S(2)}) copy-start(f32[1,768]{1,0:T(1,128)} %get-tuple-element.133) | copy-start | bytes 9220
  326.8 9.4 %copy-start.9 = (f32[4,768]{1,0:T(4,128)S(1)}, f32[4,768]{1,0:T(4,128)}, u32[]{:S(2)}) copy-start(f32[4,768]{1,0:T(4,128)} %get-tuple-element.102) | copy-start | bytes 36868
  326.8 10.0 %copy-start.2 = (f32[4,192,512]{2,1,0:T(8,128)S(1)}, f32[4,192,512]{2,1,0:T(8,128)}, u32[]{:S(2)}) copy-start(f32[4,192,512]{2,1,0:T(8,128)} %get-tuple-element.103) | copy-start | bytes 4718596
  327.6 10.4 %copy-start.1 = (f32[4,192,512]{2,1,0:T(8,128)S(1)}, f32[4,192,512]{2,1,0:T(8,128)}, u32[]{:S(2)}) copy-start(f32[4,192,512]{2,1,0:T(8,128)} %get-tuple-element.104) | copy-start | bytes 4718596
  336.8 2.3 copy-start
  337.9 2.3 copy-start.5
  337.9 3.0 copy-start.4
  339.1 2.6 copy-start.3
